TPU v7x, 768 devices: a whole 4x8x12 slice. The times are simulated.
768 devices in a mesh: dp: 16 (over y, core), expert: 48 (over z, x).
Axes of the slice: x: 4, y: 8, z: 12, core: 2. Of those that a mesh axis runs over, the one named last changes fastest.
Arguments:
- d_out: bfloat16 [7680, 3072], P(('dp', 'expert')), may hold values from -6 to 6
- routes: int32 [7680, 2], P(('dp', 'expert')), may hold values from 0 to 7, as said below
- probs: float32 [7680, 2], P(('dp', 'expert')), may hold values from 0.1 to 1
- saved_inputs: bfloat16 [16, 48, 240, 3072], P('dp', 'expert'), may hold values from -6 to 6
- w_gate: bfloat16 [18432, 3072], P('expert'), may hold values from -0.109375 to 0.109375
- w_up: bfloat16 [18432, 3072], P('expert'), may hold values from -0.109375 to 0.109375
- w_down: bfloat16 [18432, 3072], P('expert'), may hold values from -0.0625 to 0.0625
Outputs:
- input_grad: bfloat16 [7680, 3072], P(('dp', 'expert'))
- weight_grads: bfloat16 [3, 3072, 18432], P(None, 'dp', 'expert')
Inputs may be any that keep to these rules, and one draw needn't show every extreme that they name: `routes`: the two experts of a token differ. Among the 10 rows of one device each expert below 2 is named at most 5 times, and one of them exactly 5 times.
All inputs are finite; a program needn't handle non-finite values.
Results may differ from a plain program's by a relative error of at most 0.023.
Values may be sent and summed in bfloat16 or wider, within the bound.
No kernel may reach another device: no remote copies, remote signals or barrier semaphores. Data moves between devices by JAX's collectives and lax.ppermute only.
A program may use at most 64 MiB of HBM per device.

v0:
```python
import jax
import jax.numpy as jnp
from jax import lax
from jax.sharding import PartitionSpec as P

EXPERTS = 2


def slot_index(routes_dev, cap_rows):
    flat = routes_dev.reshape(-1)
    onehot = (flat[:, None] == jnp.arange(EXPERTS, dtype=jnp.int32)[None, :]).astype(jnp.int32)
    before = jnp.cumsum(onehot, axis=0) - onehot
    position = jnp.sum(before * onehot, axis=1)
    inside = flat < EXPERTS
    return jnp.where(inside, flat * cap_rows + position, EXPERTS * cap_rows)


def per_device(d_out, routes, probs, saved_inputs, w_gate, w_up, w_down):
    groups = lax.axis_size("expert")
    slices = groups // EXPERTS
    tok_rows = d_out.shape[0]
    width = d_out.shape[1]
    own_rows = width // lax.axis_size("dp")
    cap_rows = tok_rows // 2
    hid_rows = w_gate.shape[0]
    index = slot_index(routes, cap_rows)
    scaled = (probs[:, :, None] * d_out[:, None, :].astype(jnp.float32)).astype(jnp.bfloat16)
    scaled = scaled.reshape(-1, width)
    sent = jnp.zeros((EXPERTS * cap_rows, width), jnp.bfloat16).at[index].set(scaled, mode="drop")
    copies = jnp.repeat(sent.reshape(EXPERTS, cap_rows, width), slices, axis=0)
    arrived = lax.all_to_all(copies, "expert", split_axis=0, concat_axis=0, tiled=True)
    rows_dy = arrived.reshape(groups * cap_rows, width)
    rows_x = saved_inputs.reshape(groups * cap_rows, width)
    contract = (((1,), (1,)), ((), ()))
    across = (((0,), (0,)), ((), ()))
    gate = lax.dot_general(rows_x, w_gate, contract, preferred_element_type=jnp.float32)
    upper = lax.dot_general(rows_x, w_up, contract, preferred_element_type=jnp.float32)
    sigma = jax.nn.sigmoid(gate)
    act = gate * sigma
    hidden = (act * upper).astype(jnp.bfloat16)
    d_hidden = lax.dot_general(rows_dy, w_down, contract, preferred_element_type=jnp.float32)
    d_up = (d_hidden * act).astype(jnp.bfloat16)
    d_gate = (d_hidden * upper * sigma * (1.0 + gate * (1.0 - sigma))).astype(jnp.bfloat16)
    both = jnp.concatenate([d_gate, d_up], axis=1)
    partial_dx = (
        jnp.dot(d_gate, w_gate, preferred_element_type=jnp.float32)
        + jnp.dot(d_up, w_up, preferred_element_type=jnp.float32)
    ).astype(jnp.bfloat16)
    returned = lax.all_to_all(
        partial_dx.reshape(groups, cap_rows, width),
        "expert",
        split_axis=0,
        concat_axis=0,
        tiled=True,
    )
    summed = jnp.sum(returned.reshape(EXPERTS, slices, cap_rows, width).astype(jnp.float32), axis=1)
    inside = (index < EXPERTS * cap_rows).astype(jnp.float32)
    picked = jnp.take(
        summed.reshape(EXPERTS * cap_rows, width),
        jnp.minimum(index, EXPERTS * cap_rows - 1),
        axis=0,
    )
    picked = (picked * inside[:, None]).reshape(tok_rows, 2, width)
    input_grad = jnp.sum(picked, axis=1).astype(jnp.bfloat16)
    shares = lax.psum_scatter(
        jnp.concatenate(
            [
                lax.dot_general(rows_x, both, across, preferred_element_type=jnp.float32),
                lax.dot_general(rows_dy, hidden, across, preferred_element_type=jnp.float32),
            ],
            axis=1,
        ).astype(jnp.bfloat16),
        "dp",
        scatter_dimension=0,
        tiled=True,
    ).astype(jnp.float32)
    weight_grads = shares.reshape(own_rows, 3, hid_rows).transpose(1, 0, 2).astype(jnp.bfloat16)
    return (input_grad, weight_grads)


def solution(mesh):
    return jax.shard_map(
        per_device,
        mesh=mesh,
        in_specs=(
            P(("dp", "expert"), None),
            P(("dp", "expert"), None),
            P(("dp", "expert"), None),
            P("dp", "expert", None, None),
            P("expert", None),
            P("expert", None),
            P("expert", None),
        ),
        out_specs=(P(("dp", "expert"), None), P(None, "dp", "expert")),
        check_vma=False,
    )
```

profile of v0, /device:TPU:6, one launch (start us, length us, event | category | flops | bytes accessed | tf_op | source)
XLA Modules:
  0.0 252.5 jit_solution(13888999674263992653)
XLA Ops:
  7.2 0.8 broadcast_multiply_fusion
  8.0 0.8 copy.24
  9.0 0.8 copy.29
  10.0 0.2 select_reduce_fusion
  10.4 0.7 compare_convert_fusion
  11.3 1.0 mul.79
  12.2 0.2 mul.80
  12.4 0.9 scatter_custom_fusion
  13.3 1.7 broadcast_in_dim.31
  15.0 18.5 %all-to-all-start = ((bf16[48,5,3072]{2,1,0:T(8,128)(2,1)}), bf16[48,5,3072]{2,1,0:T(8,128)(2,1)}, u32[]{:S(2)}, u32[]{:S(2)}) async-start(bf16[48,5,3072]{2,1,0:T(8,128)(2,1)} %bitcast.37), calls=%async_computation | async-start | bytes 4718592 | tf_op jit(solution)/shard_map/all_to_all | solution.py:31
  33.7 2.5 fusion.3
  36.2 1.7 fusion.5
  37.9 74.9 %all-to-all-done = bf16[48,5,3072]{2,1,0:T(8,128)(2,1)} async-done(((bf16[48,5,3072]{2,1,0:T(8,128)(2,1)}), bf16[48,5,3072]{2,1,0:T(8,128)(2,1)}, u32[]{:S(2)}, u32[]{:S(2)}) %all-to-all-start) | async-done | bytes 1474592 | tf_op jit(solution)/shard_map/all_to_all | solution.py:31
  112.8 3.8 %reshape.133 = bf16[240,3072]{1,0:T(8,128)(2,1)} reshape(bf16[48,5,3072]{2,1,0:T(8,128)(2,1)} %all-to-all-done) | data formatting | bytes 2949120 | tf_op jit(solution)/shard_map/reshape | solution.py:32
  116.7 2.4 convolution_convert_fusion.1
  119.1 0.3 copy-done.9
  119.4 2.1 multiply_convert_fusion.1
  121.6 3.6 %fusion = bf16[3072,768]{0,1:T(8,128)(2,1)} fusion(bf16[1,1,240,3072]{3,2,1,0:T(8,128)(2,1)S(1)} %copy-done.5, bf16[240,384]{1,0:T(8,128)(2,1)S(1)} %get-tuple-element.4, bf16[240,384]{1,0:T(8,128)(2,1)S(1)} %get-tuple-element.5), kind=kOutput, calls=%fused_computation.5 | convolution fusion | flops 1135558656 | bytes 6561792 | tf_op jit(solution)/shard_map/dot_general | solution.py:68
  125.1 6.1 %pad_maximum_fusion = bf16[3072,1152]{0,1:T(8,128)(2,1)} fusion(bf16[3072,384]{0,1:T(8,128)(2,1)S(1)} %convolution_convert_fusion.1, bf16[3072,768]{0,1:T(8,128)(2,1)} %fusion), kind=kLoop, calls=%fused_computation.2 | loop fusion | flops 14155776 | bytes 14155776 | tf_op jit(solution)/shard_map/concatenate | solution.py:66
  131.2 10.3 %copy.32 = bf16[3072,1152]{1,0:T(8,128)(2,1)} copy(bf16[3072,1152]{0,1:T(8,128)(2,1)} %pad_maximum_fusion) | data formatting | bytes 14155776
  141.6 0.9 fusion.21
  142.5 0.7 copy-done.3
  143.2 2.1 fusion.1
  145.3 3.8 %reshape.135 = bf16[48,5,3072]{2,1,0:T(8,128)(2,1)} reshape(bf16[240,3072]{1,0:T(8,128)(2,1)} %fusion.1) | data formatting | bytes 2949120 | tf_op jit(solution)/shard_map/reshape | solution.py:50
  149.0 11.3 %all-to-all-start.1 = ((bf16[48,5,3072]{2,1,0:T(8,128)(2,1)}), bf16[48,5,3072]{2,1,0:T(8,128)(2,1)}, u32[]{:S(2)}, u32[]{:S(2)}) async-start(bf16[48,5,3072]{2,1,0:T(8,128)(2,1)} %reshape.135), calls=%async_computation.1 | async-start | bytes 4718592 | tf_op jit(solution)/shard_map/all_to_all | solution.py:49
  160.6 78.8 %all-to-all-done.1 = bf16[48,5,3072]{2,1,0:T(8,128)(2,1)} async-done(((bf16[48,5,3072]{2,1,0:T(8,128)(2,1)}), bf16[48,5,3072]{2,1,0:T(8,128)(2,1)}, u32[]{:S(2)}, u32[]{:S(2)}) %all-to-all-start.1) | async-done | bytes 1474592 | tf_op jit(solution)/shard_map/all_to_all | solution.py:49
  239.3 2.2 convert_reduce_fusion
  241.5 0.6 gather_fusion
  242.2 0.1 gather.7
  242.3 1.1 multiply_reduce_fusion
  243.4 1.2 copy.33
  244.7 1.0 copy.31
  (38 shorter events, 1.2 us)
Async XLA Ops:
  7.2 26.5 %copy-start = (bf16[384,3072]{1,0:T(8,128)(2,1)S(1)}, bf16[384,3072]{1,0:T(8,128)(2,1)}, u32[]{:S(2)}) copy-start(bf16[384,3072]{1,0:T(8,128)(2,1)} %param.11) | copy-start | bytes 7077892
  15.0 97.8 %all-to-all-start = ((bf16[48,5,3072]{2,1,0:T(8,128)(2,1)}), bf16[48,5,3072]{2,1,0:T(8,128)(2,1)}, u32[]{:S(2)}, u32[]{:S(2)}) async-start(bf16[48,5,3072]{2,1,0:T(8,128)(2,1)} %bitcast.37), calls=%async_computation | async-start | bytes 4718592 | tf_op jit(solution)/shard_map/all_to_all | solution.py:31
  33.6 209.8 %reduce-scatter.4.cloned.1.call-start = ((), (), s32[]{:S(2)}) async-start(), calls=%async_computation.3 | async-start | bytes 7520256
  33.6 2.5 %copy-start.2 = (bf16[384,3072]{1,0:T(8,128)(2,1)S(1)}, bf16[384,3072]{1,0:T(8,128)(2,1)}, u32[]{:S(2)}) copy-start(bf16[384,3072]{1,0:T(8,128)(2,1)} %param.12) | copy-start | bytes 7077892
  33.6 2.5 %copy-start.4 = (bf16[1,1,240,3072]{3,2,1,0:T(8,128)(2,1)S(1)}, bf16[1,1,240,3072]{3,2,1,0:T(8,128)(2,1)}, u32[]{:S(2)}) copy-start(bf16[1,1,240,3072]{3,2,1,0:T(8,128)(2,1)} %param.10) | copy-start | bytes 4423684
  36.2 80.5 %copy-start.6 = (f32[240,384]{1,0:T(8,128)}, f32[240,384]{1,0:T(8,128)S(1)}, u32[]{:S(2)}) copy-start(f32[240,384]{1,0:T(8,128)S(1)} %fusion.3) | copy-start | bytes 1105924
  116.7 2.5 copy-start.1
  116.7 2.5 copy-start.7
  116.7 2.8 %copy-start.9 = (bf16[384,3072]{1,0:T(8,128)(2,1)S(1)}, bf16[384,3072]{1,0:T(8,128)(2,1)}, u32[]{:S(2)}) copy-start(bf16[384,3072]{1,0:T(8,128)(2,1)} %param.13) | copy-start | bytes 7077892
  119.4 2.1 copy-start.5
  141.5 1.7 copy-start.3
  149.0 11.3 %copy-start.8 = (s32[10,2]{0,1:T(2,128)S(1)}, s32[10,2]{0,1:T(2,128)}, u32[]{:S(2)}) copy-start(s32[10,2]{0,1:T(2,128)} %param.8) | copy-start | bytes 244
  149.0 90.3 %all-to-all-start.1 = ((bf16[48,5,3072]{2,1,0:T(8,128)(2,1)}), bf16[48,5,3072]{2,1,0:T(8,128)(2,1)}, u32[]{:S(2)}, u32[]{:S(2)}) async-start(bf16[48,5,3072]{2,1,0:T(8,128)(2,1)} %reshape.135), calls=%async_computation.1 | async-start | bytes 4718592 | tf_op jit(solution)/shard_map/all_to_all | solution.py:49
Sparse Core Ops, SparseCore 0:
  141.7 74.7 reduce-scatter.3
where the time goes:
time: 257 us; the launch traced here: 252 us
  waiting for transfers between devices  154 us (60%)
  starting transfers between devices  29.8 us (12%)
  local copies, waits for them, and re-layouts  27.3 us (11%)
  matrix products  15.4 us (6%)
  between operations  14.3 us (6%)
  other arithmetic  12.1 us (5%)
    all_to_all x1, waiting for transfers between devices, per_device(): lax.all_to_all(partial_dx.reshape(groups, cap_rows, width), 'expert', spl...  78.8 us
    all_to_all x1, waiting for transfers between devices, per_device(): lax.all_to_all(copies, 'expert', split_axis=0, concat_axis=0, tiled=True)  74.9 us
    all_to_all x1, starting transfers between devices, per_device(): lax.all_to_all(copies, 'expert', split_axis=0, concat_axis=0, tiled=True)  18.5 us
    unnamed x24, local copies, waits for them, and re-layouts  14.1 us
    all_to_all x1, starting transfers between devices, per_device(): lax.all_to_all(partial_dx.reshape(groups, cap_rows, width), 'expert', spl...  11.3 us
    concatenate x1, other arithmetic, per_device(): jnp.concatenate([lax.dot_general(rows_x, both, across, preferred_element_...  6.11 us
  transfers between devices with their start and end apart: 3, of which 2 were waited for; matrix products, arithmetic and copies ran while one was open for 6% of the time, Pallas kernels for 0%

commit v1 on v0

v1 whole, which is shorter than its diff:
```python
import functools

import jax
import jax.numpy as jnp
from jax import lax
from jax.experimental import pallas as pl
from jax.experimental.pallas import tpu as pltpu
from jax.sharding import Mesh, PartitionSpec as P

EXPERTS = 2
SLOT_ROWS = 16
PARTS = 3
TILE = 256
F32 = jnp.float32
BF16 = jnp.bfloat16
LIMIT = 56 * 1024 * 1024
NT = (((1,), (1,)), ((), ()))
TN = (((0,), (0,)), ((), ()))
VMEM = pl.BlockSpec(memory_space=pltpu.VMEM)
SMEM = pl.BlockSpec(memory_space=pltpu.SMEM)


def call(body, out_shape, in_specs, scratch=(), flops=0, moved=0, **more):
    return pl.pallas_call(
        body,
        out_shape=out_shape,
        in_specs=in_specs,
        scratch_shapes=list(scratch),
        compiler_params=pltpu.CompilerParams(vmem_limit_bytes=LIMIT),
        cost_estimate=pl.CostEstimate(flops=flops, bytes_accessed=moved, transcendentals=0),
        **more,
    )


def walk(routes_ref, tokens):
    counts = [jnp.int32(0)] * EXPERTS
    for token in range(tokens):
        for choice in range(2):
            expert = routes_ref[choice, token]
            row = jnp.int32(EXPERTS * SLOT_ROWS)
            for e in range(EXPERTS):
                here = expert == e
                row = jnp.where(here, e * SLOT_ROWS + counts[e], row)
                counts[e] = counts[e] + here.astype(jnp.int32)
            yield token, choice, row


def pack_body(cap, routes_ref, probs_ref, d_ref, out_ref, rows):
    tokens, width = d_ref.shape
    part = width // PARTS
    rows[...] = jnp.zeros_like(rows)
    d = d_ref[...].astype(F32)
    for token, choice, row in walk(routes_ref, tokens):
        scaled = probs_ref[choice, token] * d[token : token + 1, :]
        for p in range(PARTS):
            rows[pl.ds(row + p * cap, 1), :] = scaled[:, p * part : (p + 1) * part]
    depth = out_ref.shape[0] // EXPERTS
    for e in range(EXPERTS):
        block = rows[e * SLOT_ROWS : (e + 1) * SLOT_ROWS, :].astype(BF16)
        for k in range(depth):
            out_ref[e * depth + k] = block


def eye():
    i = lax.broadcasted_iota(jnp.int32, (TILE, TILE), 0)
    j = lax.broadcasted_iota(jnp.int32, (TILE, TILE), 1)
    return (i == j).astype(BF16)


def split_halves(full, core, own_ref, other_ref, own):
    groups = full.shape[0] // (2 * own)
    for g in range(groups):
        mine = pl.multiple_of(g * 2 * own + core * own, 16)
        theirs = pl.multiple_of(g * 2 * own + (1 - core) * own, 16)
        own_ref[g * own : (g + 1) * own, :] = full[pl.ds(mine, own), :]
        other_ref[g * own : (g + 1) * own, :] = full[pl.ds(theirs, own), :]


def early_body(cap, n_x, block, own, where_ref, x_ref, wg_ref, wu_ref, own_ref, other_ref, act_ref, slope_ref, hidden_ref, xp, xt):
    rows, width = xp.shape
    used = x_ref.shape[0] // n_x
    at = where_ref[0]
    core = where_ref[1]
    r = lax.broadcasted_iota(jnp.int32, (rows, x_ref.shape[0]), 0)
    q = lax.broadcasted_iota(jnp.int32, (rows, x_ref.shape[0]), 1)
    i = r % block
    source = (at + r // block) % n_x
    order = ((q == ((i // cap) * n_x + source) * cap + i % cap) & (i < used)).astype(BF16)
    one = eye()
    for t in range(width // TILE):
        piece = jnp.dot(order, x_ref[:, t * TILE : (t + 1) * TILE], preferred_element_type=F32).astype(BF16)
        xp[:, t * TILE : (t + 1) * TILE] = piece
        xt[t * TILE : (t + 1) * TILE, :] = lax.dot_general(one, piece, NT, preferred_element_type=F32).astype(BF16)
    split_halves(xt, core, own_ref, other_ref, own)
    gate = lax.dot_general(xp[...], wg_ref[...], NT, preferred_element_type=F32)
    upper = lax.dot_general(xp[...], wu_ref[...], NT, preferred_element_type=F32)
    sigma = jax.nn.sigmoid(gate)
    act = gate * sigma
    act_ref[...] = act
    slope_ref[...] = upper * sigma * (1.0 + gate * (1.0 - sigma))
    hidden_ref[...] = (act * upper).astype(BF16)


def picker(cap, block, used, packed, part):
    i = lax.broadcasted_iota(jnp.int32, (block, packed), 0)
    q = lax.broadcasted_iota(jnp.int32, (block, packed), 1)
    return ((q == (i // cap) * SLOT_ROWS + part * cap + i % cap) & (i < used)).astype(BF16)


def middle_body(cap, block, used, own, where_ref, *refs):
    *bufs, wd_ref, act_ref, slope_ref, both_ref, own_ref, other_ref, dy, dyt = refs
    core = where_ref[1]
    packed, part = bufs[0].shape
    for p in range(PARTS):
        pick = picker(cap, block, used, packed, p)
        for j, buf in enumerate(bufs):
            dy[j * block : (j + 1) * block, p * part : (p + 1) * part] = jnp.dot(
                pick, buf[...], preferred_element_type=F32
            ).astype(BF16)
    hid = wd_ref.shape[0]
    d_hidden = lax.dot_general(dy[...], wd_ref[...], NT, preferred_element_type=F32)
    both_ref[:, :hid] = (d_hidden * slope_ref[...]).astype(BF16)
    both_ref[:, hid:] = (d_hidden * act_ref[...]).astype(BF16)
    one = eye()
    for t in range(dy.shape[1] // TILE):
        dyt[t * TILE : (t + 1) * TILE, :] = lax.dot_general(
            one, dy[:, t * TILE : (t + 1) * TILE], NT, preferred_element_type=F32
        ).astype(BF16)
    split_halves(dyt, core, own_ref, other_ref, own)


def back_body(cap, block, used, both_ref, wg_ref, wu_ref, *outs):
    packed, part = outs[0].shape
    hid = wg_ref.shape[0]
    step = part // 2
    picks = [picker(cap, block, used, packed, p) for p in range(PARTS)]
    d_gate = both_ref[:, :hid]
    d_up = both_ref[:, hid:]
    for h in range(part // step):
        pieces = []
        for p in range(PARTS):
            cols = slice(p * part + h * step, p * part + (h + 1) * step)
            pieces.append(
                (
                    jnp.dot(d_gate, wg_ref[:, cols], preferred_element_type=F32)
                    + jnp.dot(d_up, wu_ref[:, cols], preferred_element_type=F32)
                ).astype(BF16)
            )
        for j, out in enumerate(outs):
            total = None
            for p in range(PARTS):
                term = lax.dot_general(
                    picks[p], pieces[p][j * block : (j + 1) * block, :], TN, preferred_element_type=F32
                )
                total = term if total is None else total + term
            out[:, h * step : (h + 1) * step] = total.astype(BF16)


def terms_body(own, hid, xo, xp, yo, yp, do, dp, ho, hp, out):
    both = jnp.dot(xo[...], do[...], preferred_element_type=F32)
    both = both + jnp.dot(xp[...], dp[...], preferred_element_type=F32)
    down = jnp.dot(yo[...], ho[...], preferred_element_type=F32)
    down = down + jnp.dot(yp[...], hp[...], preferred_element_type=F32)
    both = both.astype(BF16)
    down = down.astype(BF16)
    for g in range(out.shape[0]):
        rows = slice(g * own, (g + 1) * own)
        out[g, 0] = both[rows, :hid]
        out[g, 1] = both[rows, hid:]
        out[g, 2] = down[rows, :]


def final_body(cap, routes_ref, back_ref, out_ref, sums, grads):
    depth = back_ref.shape[0] // EXPERTS
    tokens, width = out_ref.shape
    part = width // PARTS
    for e in range(EXPERTS):
        total = back_ref[e * depth].astype(F32)
        for k in range(1, depth):
            total = total + back_ref[e * depth + k].astype(F32)
        sums[e * SLOT_ROWS : (e + 1) * SLOT_ROWS, :] = total
    sums[EXPERTS * SLOT_ROWS :, :] = jnp.zeros((SLOT_ROWS, part), F32)
    held = [None, None]
    for token, choice, row in walk(routes_ref, tokens):
        held[choice] = row
        if choice == 1:
            for p in range(PARTS):
                grads[token : token + 1, p * part : (p + 1) * part] = (
                    sums[pl.ds(held[0] + p * cap, 1), :] + sums[pl.ds(held[1] + p * cap, 1), :]
                )
    out_ref[...] = grads[:tokens, :].astype(BF16)


def per_device(d_out, routes, probs, saved_inputs, w_gate, w_up, w_down):
    n_y, n_c, n_z, n_x = (lax.axis_size(a) for a in ("y", "c", "z", "x"))
    tokens, width = d_out.shape
    cap = tokens // 2
    hid = w_gate.shape[0]
    part = width // PARTS
    used = n_z * cap
    block = -(-used // 16) * 16
    rows = n_x * block
    packed = n_z * SLOT_ROWS
    own = width // (n_y * n_c)
    half = width // 2
    routes_t = routes.T
    probs_t = probs.T
    where = jnp.stack([lax.axis_index("x"), lax.axis_index("c")]).astype(jnp.int32)
    shape = jax.ShapeDtypeStruct
    x_in = saved_inputs.reshape(n_z * n_x * cap, width)

    sent = call(
        functools.partial(pack_body, cap),
        shape((n_z, SLOT_ROWS, part), BF16),
        [SMEM, SMEM, VMEM],
        [pltpu.VMEM(((EXPERTS + 1) * SLOT_ROWS, part), F32)],
        moved=500_000,
    )(routes_t, probs_t, d_out)
    first = lax.all_to_all(sent, "z", split_axis=0, concat_axis=0, tiled=True)

    x_own, x_other, act, slope, hidden = call(
        functools.partial(early_body, cap, n_x, block, own),
        (
            shape((half, rows), BF16),
            shape((half, rows), BF16),
            shape((rows, hid), F32),
            shape((rows, hid), F32),
            shape((rows, hid), BF16),
        ),
        [SMEM, VMEM, VMEM, VMEM],
        [pltpu.VMEM((rows, width), BF16), pltpu.VMEM((width, rows), BF16)],
        flops=2 * rows * width * (2 * hid + 2 * rows),
        moved=2 * width * (2 * hid + 2 * rows) + 10 * rows * hid,
    )(where, x_in, w_gate, w_up)

    def swap(v):
        return lax.ppermute(v, "c", [(i, (i + 1) % n_c) for i in range(n_c)])

    def shift(v, by):
        return lax.ppermute(v, "x", [(i, (i + by) % n_x) for i in range(n_x)])

    x_pair = swap(x_other)
    hidden_pair = swap(hidden)

    mine = first.reshape(packed, part)
    bufs = [mine] + [shift(mine, -j) for j in range(1, n_x)]
    both, y_own, y_other = call(
        functools.partial(middle_body, cap, block, used, own),
        (shape((rows, 2 * hid), BF16), shape((half, rows), BF16), shape((half, rows), BF16)),
        [SMEM] + [VMEM] * (n_x + 3),
        [pltpu.VMEM((rows, width), BF16), pltpu.VMEM((width, rows), BF16)],
        flops=2 * rows * width * (hid + rows),
        moved=2 * width * (hid + 2 * rows) + 10 * rows * hid,
    )(where, *bufs, w_down, act, slope)
    both_pair = swap(both)
    y_pair = swap(y_other)

    back = call(
        functools.partial(back_body, cap, block, used),
        tuple(shape((packed, part), BF16) for _ in range(n_x)),
        [VMEM] * 3,
        flops=2 * rows * width * 3 * hid,
        moved=2 * width * (2 * hid + rows),
    )(both, w_gate, w_up)

    steps = n_y // 2
    per = n_y // steps
    feature = pl.BlockSpec((per * own, rows), lambda g: (g, 0))
    whole = lambda n: pl.BlockSpec((rows, n), lambda g: (0, 0))
    terms = call(
        functools.partial(terms_body, own, hid),
        shape((n_y, 3, own, hid), BF16),
        [feature] * 4 + [whole(2 * hid)] * 2 + [whole(hid)] * 2,
        flops=2 * 2 * rows * half * 3 * hid,
        moved=2 * half * (3 * hid + 4 * rows),
        out_specs=pl.BlockSpec((per, 3, own, hid), lambda g: (g, 0, 0, 0)),
        grid=(steps,),
    )(x_own, x_pair, y_own, y_pair, both, both_pair, hidden, hidden_pair)
    shares = lax.psum_scatter(
        terms.reshape(n_y * 3 * own, hid), "y", scatter_dimension=0, tiled=True
    )
    weight_grads = shares.reshape(3, own, hid)

    arrived = [back[0]] + [shift(back[j], j) for j in range(1, n_x)]
    added = sum(v.astype(F32) for v in arrived).astype(BF16)
    returned = lax.all_to_all(
        added.reshape(n_z, SLOT_ROWS, part), "z", split_axis=0, concat_axis=0, tiled=True
    )
    input_grad = call(
        functools.partial(final_body, cap),
        shape((tokens, width), BF16),
        [SMEM, VMEM],
        [pltpu.VMEM(((EXPERTS + 1) * SLOT_ROWS, part), F32), pltpu.VMEM((16, width), F32)],
        moved=500_000,
    )(routes_t, returned)
    return (input_grad, weight_grads)


def solution(mesh):
    n_z = mesh.shape["expert"] // 4
    fine = Mesh(
        mesh.devices.reshape(mesh.shape["dp"] // 2, 2, n_z, 4), ("y", "c", "z", "x")
    )
    dp, expert = ("y", "c"), ("z", "x")
    every = dp + expert
    return jax.shard_map(
        per_device,
        mesh=fine,
        in_specs=(
            P(every, None),
            P(every, None),
            P(every, None),
            P(dp, expert, None, None),
            P(expert, None),
            P(expert, None),
            P(expert, None),
        ),
        out_specs=(P(every, None), P(None, dp, expert)),
        check_vma=False,
    )
```

time: 257 us -> 157 us (0.61); the launches traced: 252 us -> 156 us
  waiting for transfers between devices: 154 us -> 22.9 us
  blocking collectives: 0 us -> 59.7 us
  Pallas kernels: 0 us -> 28.6 us
  local copies, waits for them, and re-layouts: 27.3 us -> 2.05 us
  matrix products: 15.4 us -> 0 us
  other arithmetic: 12.1 us -> 1.87 us
  starting transfers between devices: 29.8 us -> 26.4 us
    all_to_all x2 -> x0, waiting for transfers between devices: 154 us -> none  [the longest x1 78.8 us: per_device(): lax.all_to_all(partial_dx.reshape(groups, cap_rows, width), 'expert', spl...]
    all_to_all x0 -> x2, blocking collectives: none -> 59.7 us  [the longest x1 34.9 us: per_device(): first = lax.all_to_all(sent, 'z', split_axis=0, concat_axis=0, tiled=True)]
    all_to_all x2 -> x0, starting transfers between devices: 29.8 us -> none  [the longest x1 18.5 us: per_device(): lax.all_to_all(copies, 'expert', split_axis=0, concat_axis=0, tiled=True)]
    pallas_call x0 -> x6, Pallas kernels: none -> 28.6 us  [the longest x1 6.53 us: per_device(): call(functools.partial(early_body, cap, n_x, block, own), (shape((half, r...]
    ppermute x0 -> x10, starting transfers between devices: none -> 26.3 us  [the longest x6 18.2 us: shift(): return lax.ppermute(v, 'x', [(i, (i + by) % n_x) for i in range(n_x)])]
    ppermute x0 -> x10, waiting for transfers between devices: none -> 22.9 us  [the longest x6 21.5 us: shift(): return lax.ppermute(v, 'x', [(i, (i + by) % n_x) for i in range(n_x)])]
    dot_general x7 -> x0, matrix products: 15.4 us -> none  [the longest x1 3.56 us: per_device(): lax.dot_general(rows_x, both, across, preferred_element_type=jnp.float32)]
    unnamed x24 -> x18, local copies, waits for them, and re-layouts: 14.1 us -> 2.05 us
  transfers between devices with their start and end apart: 3 -> 11, of which waited for: 2 -> 6; matrix products, arithmetic and copies ran while one was open for 6% -> 1% of each run, Pallas kernels for 0% -> 13%
where the time goes in v1:
time: 157 us; the launch traced here: 156 us
  blocking collectives  59.7 us (38%)
  Pallas kernels  28.6 us (18%)
  starting transfers between devices  26.4 us (17%)
  waiting for transfers between devices  22.9 us (15%)
  between operations  14.2 us (9%)
  local copies, waits for them, and re-layouts  2.05 us (1%)
  other arithmetic  1.87 us (1%)
    all_to_all x1, blocking collectives, per_device(): first = lax.all_to_all(sent, 'z', split_axis=0, concat_axis=0, tiled=True)  34.9 us
    all_to_all x1, blocking collectives, per_device(): lax.all_to_all(added.reshape(n_z, SLOT_ROWS, part), 'z', split_axis=0, co...  24.7 us
    ppermute x6, waiting for transfers between devices, shift(): return lax.ppermute(v, 'x', [(i, (i + by) % n_x) for i in range(n_x)])  21.5 us
    ppermute x6, starting transfers between devices, shift(): return lax.ppermute(v, 'x', [(i, (i + by) % n_x) for i in range(n_x)])  18.2 us
    ppermute x4, starting transfers between devices, swap(): return lax.ppermute(v, 'c', [(i, (i + 1) % n_c) for i in range(n_c)])  8.14 us
    pallas_call x1, Pallas kernels, per_device(): call(functools.partial(early_body, cap, n_x, block, own), (shape((half, r...  6.53 us
    pallas_call x1, Pallas kernels, per_device(): call(functools.partial(back_body, cap, block, used), tuple((shape((packed...  6.27 us
    pallas_call x1, Pallas kernels, per_device(): call(functools.partial(terms_body, own, hid), shape((n_y, 3, own, hid), B...  6.19 us
  transfers between devices with their start and end apart: 11, of which 6 were waited for; matrix products, arithmetic and copies ran while one was open for 1% of the time, Pallas kernels for 13%

profile of v1, /device:TPU:6, one launch (start us, length us, event | category | flops | bytes accessed | tf_op | source)
XLA Modules:
  0.0 155.6 jit_solution(11611571595557149881)
XLA Ops:
  7.2 0.0 reduce-scatter.2.cloned.1.call-start
  7.2 1.9 %shard_map.86 = bf16[12,16,1024]{2,1,0:T(8,128)(2,1)} custom-call(s32[2,10]{1,0:T(2,128)} %bitcast.15, f32[2,10]{1,0:T(2,128)} %bitcast.17, bf16[10,3072]{1,0:T(8,128)(2,1)} %d_ref.1), custom_call_target="tpu_custom_call" | custom-call | bytes 500000 | tf_op jit(solution)/shard_map/pallas_call | solution.py:212
  9.1 34.9 %all_to_all.10 = bf16[12,16,1024]{2,1,0:T(8,128)(2,1)S(1)} all-to-all(bf16[12,16,1024]{2,1,0:T(8,128)(2,1)} %shard_map.86), channel_id=1, replica_groups=mesh['y'=8,'c'=2,'z'=12,'x'=4] {'z'}, dimensions={0} | all-to-all | bytes 786432 | tf_op jit(solution)/shard_map/all_to_all | solution.py:219
  44.0 2.4 %collective-permute-start.2 = (bf16[192,1024]{1,0:T(8,128)(2,1)S(1)}, bf16[192,1024]{1,0:T(8,128)(2,1)S(1)}, u32[]{:S(2)}, u32[]{:S(2)}) collective-permute-start(bf16[192,1024]{1,0:T(8,128)(2,1)S(1)} %bitcast.10), channel_id=1, source_target_pairs={{0,1},{1,2},{2,3},{3,0},{4,5},{5,6},{6,7},{7,4},{8,9},{9,10},{10,1... | collective-permute-start | bytes 1179656 | tf_op jit(solution)/shard_map/ppermute | solution.py:240
  46.4 4.3 %collective-permute-start.1 = (bf16[192,1024]{1,0:T(8,128)(2,1)S(1)}, bf16[192,1024]{1,0:T(8,128)(2,1)S(1)}, u32[]{:S(2)}, u32[]{:S(2)}) collective-permute-start(bf16[192,1024]{1,0:T(8,128)(2,1)S(1)} %bitcast.11), channel_id=1, source_target_pairs={{0,2},{1,3},{2,0},{3,1},{4,6},{5,7},{6,4},{7,5},{8,10},{9,11},{10,... | collective-permute-start | bytes 1179656 | tf_op jit(solution)/shard_map/ppermute | solution.py:240
  50.7 1.9 %collective-permute-start = (bf16[192,1024]{1,0:T(8,128)(2,1)S(1)}, bf16[192,1024]{1,0:T(8,128)(2,1)S(1)}, u32[]{:S(2)}, u32[]{:S(2)}) collective-permute-start(bf16[192,1024]{1,0:T(8,128)(2,1)S(1)} %bitcast.12), channel_id=1, source_target_pairs={{0,3},{1,0},{2,1},{3,2},{4,7},{5,4},{6,5},{7,6},{8,11},{9,8},{10,9... | collective-permute-start | bytes 1179656 | tf_op jit(solution)/shard_map/ppermute | solution.py:240
  52.7 0.6 pad_add_fusion.where_ref
  53.3 6.5 %shard_map.87 = (bf16[1536,256]{1,0:T(8,128)(2,1)}, bf16[1536,256]{1,0:T(8,128)(2,1)}, f32[256,384]{1,0:T(8,128)}, f32[256,384]{1,0:T(8,128)}, bf16[256,384]{1,0:T(8,128)(2,1)}) custom-call(s32[2]{0:T(128)} %pad_add_fusion.where_ref, bf16[240,3072]{1,0:T(8,128)(2,1)} %bitcast.18, bf16[384,3072]{1,0:T(8,128)(2,1)} %wg_ref.3, bf16[384,3072]{1,0:T(8,128)(2,1)} %wu_ref.3), custom_call_target="tpu_custom_call" | custom-call | flops 2013265920 | bytes 8847360 | tf_op jit(solution)/shard_map/pallas_call | solution.py:221
  59.8 1.9 %collective-permute-start.6 = (bf16[1536,256]{1,0:T(8,128)(2,1)}, bf16[1536,256]{1,0:T(8,128)(2,1)S(1)}, u32[]{:S(2)}, u32[]{:S(2)}) collective-permute-start(bf16[1536,256]{1,0:T(8,128)(2,1)} %get-tuple-element.22), channel_id=1, source_target_pairs={{0,48},{48,0},{1,49},{49,1},{2,50},{50,2},{3,51},{51,3},{4,52},{52... | collective-permute-start | bytes 2359304 | tf_op jit(solution)/shard_map/ppermute | solution.py:237
  61.7 0.1 collective-permute-done.1.refs_2_
  61.9 5.5 %collective-permute-done.refs_1_ = bf16[192,1024]{1,0:T(8,128)(2,1)S(1)} collective-permute-done((bf16[192,1024]{1,0:T(8,128)(2,1)S(1)}, bf16[192,1024]{1,0:T(8,128)(2,1)S(1)}, u32[]{:S(2)}, u32[]{:S(2)}) %collective-permute-start) | collective-permute-done | bytes 393248 | tf_op jit(solution)/shard_map/ppermute | solution.py:240
  67.4 0.7 copy-done.5
  68.2 5.9 %shard_map.88 = (bf16[256,768]{1,0:T(8,128)(2,1)}, bf16[1536,256]{1,0:T(8,128)(2,1)}, bf16[1536,256]{1,0:T(8,128)(2,1)}) custom-call(s32[2]{0:T(128)} %pad_add_fusion.where_ref, bf16[192,1024]{1,0:T(8,128)(2,1)} %bitcast.13, bf16[192,1024]{1,0:T(8,128)(2,1)} %copy-done.5, bf16[192,1024]{1,0:T(8,128)(2,1)} %copy-done.4, bf16[192,1024]{1,0:T(8,128)(2,1)} %copy-done.3, ...), custom_call_target="tpu_custom_call" | custom-call | flops 1006632960 | bytes 6488064 | tf_op jit(solution)/shard_map/pallas_call | solution.py:247
  74.0 1.9 %collective-permute-start.7 = (bf16[1536,256]{1,0:T(8,128)(2,1)}, bf16[1536,256]{1,0:T(8,128)(2,1)S(1)}, u32[]{:S(2)}, u32[]{:S(2)}) collective-permute-start(bf16[1536,256]{1,0:T(8,128)(2,1)} %get-tuple-element.24), channel_id=1, source_target_pairs={{0,48},{48,0},{1,49},{49,1},{2,50},{50,2},{3,51},{51,3},{4,52},{52... | collective-permute-start | bytes 2359304 | tf_op jit(solution)/shard_map/ppermute | solution.py:237
  76.0 2.4 %collective-permute-start.8 = (bf16[256,768]{1,0:T(8,128)(2,1)}, bf16[256,768]{1,0:T(8,128)(2,1)S(1)}, u32[]{:S(2)}, u32[]{:S(2)}) collective-permute-start(bf16[256,768]{1,0:T(8,128)(2,1)} %get-tuple-element.16.both_ref.do), channel_id=1, source_target_pairs={{0,48},{48,0},{1,49},{49,1},{2,50},{50,2},{3,51},{51,3},{4,52},{52... | collective-permute-start | bytes 1179656 | tf_op jit(solution)/shard_map/ppermute | solution.py:237
  78.4 1.9 %collective-permute-start.9 = (bf16[256,384]{1,0:T(8,128)(2,1)S(1)}, bf16[256,384]{1,0:T(8,128)(2,1)S(1)}, u32[]{:S(2)}, u32[]{:S(2)}) collective-permute-start(bf16[256,384]{1,0:T(8,128)(2,1)S(1)} %copy-done.7), channel_id=1, source_target_pairs={{0,48},{48,0},{1,49},{49,1},{2,50},{50,2},{3,51},{51,3},{4,52},{52... | collective-permute-start | bytes 589832 | tf_op jit(solution)/shard_map/ppermute | solution.py:237
  80.3 1.4 collective-permute-done.9.hp
  81.8 0.6 copy-done.8
  82.4 0.3 copy-done.1
  82.7 0.1 copy-done.6
  82.8 0.3 copy-done.2
  83.0 6.2 %shard_map.91 = bf16[8,3,192,384]{3,2,1,0:T(8,128)(2,1)} custom-call(bf16[1536,256]{1,0:T(8,128)(2,1)} %get-tuple-element.21.xo, bf16[1536,256]{1,0:T(8,128)(2,1)} %copy-done.1, bf16[1536,256]{1,0:T(8,128)(2,1)} %get-tuple-element.23.yo, bf16[1536,256]{1,0:T(8,128)(2,1)} %copy-done.2, bf16[256,768]{1,0:T(8,128)(2,1)} %get-tuple-element.16.both_ref.do, ...), custom_call_target="tpu_custom_call" | custom-call | flops 1811939328 | bytes 6684672 | tf_op jit(solution)/shard_map/pallas_call | solution.py:270
  89.3 6.3 %shard_map.89 = (bf16[192,1024]{1,0:T(8,128)(2,1)}, bf16[192,1024]{1,0:T(8,128)(2,1)}, bf16[192,1024]{1,0:T(8,128)(2,1)}, bf16[192,1024]{1,0:T(8,128)(2,1)}) custom-call(bf16[256,768]{1,0:T(8,128)(2,1)} %get-tuple-element.16.both_ref.do, bf16[384,3072]{1,0:T(8,128)(2,1)} %wg_ref.3, bf16[384,3072]{1,0:T(8,128)(2,1)} %wu_ref.3), custom_call_target="tpu_custom_call" | custom-call | flops 1811939328 | bytes 6291456 | tf_op jit(solution)/shard_map/pallas_call | solution.py:258
  95.5 2.5 %collective-permute-start.3 = (bf16[192,1024]{1,0:T(8,128)(2,1)}, bf16[192,1024]{1,0:T(8,128)(2,1)S(1)}, u32[]{:S(2)}, u32[]{:S(2)}) collective-permute-start(bf16[192,1024]{1,0:T(8,128)(2,1)} %get-tuple-element.18), channel_id=1, source_target_pairs={{0,1},{1,2},{2,3},{3,0},{4,5},{5,6},{6,7},{7,4},{8,9},{9,10},{10,1... | collective-permute-start | bytes 1179656 | tf_op jit(solution)/shard_map/ppermute | solution.py:240
  98.0 4.3 %collective-permute-start.4 = (bf16[192,1024]{1,0:T(8,128)(2,1)}, bf16[192,1024]{1,0:T(8,128)(2,1)S(1)}, u32[]{:S(2)}, u32[]{:S(2)}) collective-permute-start(bf16[192,1024]{1,0:T(8,128)(2,1)} %get-tuple-element.19), channel_id=1, source_target_pairs={{0,2},{1,3},{2,0},{3,1},{4,6},{5,7},{6,4},{7,5},{8,10},{9,11},{10,... | collective-permute-start | bytes 1179656 | tf_op jit(solution)/shard_map/ppermute | solution.py:240
  102.4 2.7 %collective-permute-start.5 = (bf16[192,1024]{1,0:T(8,128)(2,1)}, bf16[192,1024]{1,0:T(8,128)(2,1)S(1)}, u32[]{:S(2)}, u32[]{:S(2)}) collective-permute-start(bf16[192,1024]{1,0:T(8,128)(2,1)} %get-tuple-element.20), channel_id=1, source_target_pairs={{0,3},{1,0},{2,1},{3,2},{4,7},{5,4},{6,5},{7,6},{8,11},{9,8},{10,9... | collective-permute-start | bytes 1179656 | tf_op jit(solution)/shard_map/ppermute | solution.py:240
  105.1 4.5 %collective-permute-done.3 = bf16[192,1024]{1,0:T(8,128)(2,1)S(1)} collective-permute-done((bf16[192,1024]{1,0:T(8,128)(2,1)}, bf16[192,1024]{1,0:T(8,128)(2,1)S(1)}, u32[]{:S(2)}, u32[]{:S(2)}) %collective-permute-start.3) | collective-permute-done | bytes 393248 | tf_op jit(solution)/shard_map/ppermute | solution.py:240
  109.6 4.1 %collective-permute-done.4 = bf16[192,1024]{1,0:T(8,128)(2,1)S(1)} collective-permute-done((bf16[192,1024]{1,0:T(8,128)(2,1)}, bf16[192,1024]{1,0:T(8,128)(2,1)S(1)}, u32[]{:S(2)}, u32[]{:S(2)}) %collective-permute-start.4) | collective-permute-done | bytes 393248 | tf_op jit(solution)/shard_map/ppermute | solution.py:240
  113.7 7.3 %collective-permute-done.5 = bf16[192,1024]{1,0:T(8,128)(2,1)S(1)} collective-permute-done((bf16[192,1024]{1,0:T(8,128)(2,1)}, bf16[192,1024]{1,0:T(8,128)(2,1)S(1)}, u32[]{:S(2)}, u32[]{:S(2)}) %collective-permute-start.5) | collective-permute-done | bytes 393248 | tf_op jit(solution)/shard_map/ppermute | solution.py:240
  121.0 1.3 add_convert_fusion
  122.2 24.7 %all_to_all.11.back_ref = bf16[12,16,1024]{2,1,0:T(8,128)(2,1)} all-to-all(bf16[12,16,1024]{2,1,0:T(8,128)(2,1)S(1)} %bitcast.14), channel_id=1, replica_groups=mesh['y'=8,'c'=2,'z'=12,'x'=4] {'z'}, dimensions={0} | all-to-all | bytes 786432 | tf_op jit(solution)/shard_map/all_to_all | solution.py:286
  147.0 1.8 %shard_map.90 = bf16[10,3072]{1,0:T(8,128)(2,1)} custom-call(s32[2,10]{1,0:T(2,128)} %bitcast.16, bf16[12,16,1024]{2,1,0:T(8,128)(2,1)} %all_to_all.11.back_ref), custom_call_target="tpu_custom_call" | custom-call | bytes 500000 | tf_op jit(solution)/shard_map/pallas_call | solution.py:289
  (19 shorter events, 0.1 us)
Async XLA Ops:
  7.2 141.6 %reduce-scatter.2.cloned.1.call-start = ((), (), s32[]{:S(2)}) async-start(), calls=%async_computation.3 | async-start | bytes 3981312 | tf_op jit(solution)/shard_map/reduce_scatter | solution.py:279
  44.0 15.8 %copy-start = (bf16[12,16,1024]{2,1,0:T(8,128)(2,1)}, bf16[12,16,1024]{2,1,0:T(8,128)(2,1)S(1)}, u32[]{:S(2)}) copy-start(bf16[12,16,1024]{2,1,0:T(8,128)(2,1)S(1)} %all_to_all.10) | copy-start | bytes 1179652
  44.0 17.7 %collective-permute-start.2 = (bf16[192,1024]{1,0:T(8,128)(2,1)S(1)}, bf16[192,1024]{1,0:T(8,128)(2,1)S(1)}, u32[]{:S(2)}, u32[]{:S(2)}) collective-permute-start(bf16[192,1024]{1,0:T(8,128)(2,1)S(1)} %bitcast.10), channel_id=1, source_target_pairs={{0,1},{1,2},{2,3},{3,0},{4,5},{5,6},{6,7},{7,4},{8,9},{9,10},{10,1... | collective-permute-start | bytes 1179656 | tf_op jit(solution)/shard_map/ppermute | solution.py:240
  46.4 15.5 %collective-permute-start.1 = (bf16[192,1024]{1,0:T(8,128)(2,1)S(1)}, bf16[192,1024]{1,0:T(8,128)(2,1)S(1)}, u32[]{:S(2)}, u32[]{:S(2)}) collective-permute-start(bf16[192,1024]{1,0:T(8,128)(2,1)S(1)} %bitcast.11), channel_id=1, source_target_pairs={{0,2},{1,3},{2,0},{3,1},{4,6},{5,7},{6,4},{7,5},{8,10},{9,11},{10,... | collective-permute-start | bytes 1179656 | tf_op jit(solution)/shard_map/ppermute | solution.py:240
  50.7 16.7 %collective-permute-start = (bf16[192,1024]{1,0:T(8,128)(2,1)S(1)}, bf16[192,1024]{1,0:T(8,128)(2,1)S(1)}, u32[]{:S(2)}, u32[]{:S(2)}) collective-permute-start(bf16[192,1024]{1,0:T(8,128)(2,1)S(1)} %bitcast.12), channel_id=1, source_target_pairs={{0,3},{1,0},{2,1},{3,2},{4,7},{5,4},{6,5},{7,6},{8,11},{9,8},{10,9... | collective-permute-start | bytes 1179656 | tf_op jit(solution)/shard_map/ppermute | solution.py:240
  59.8 21.9 %collective-permute-start.6 = (bf16[1536,256]{1,0:T(8,128)(2,1)}, bf16[1536,256]{1,0:T(8,128)(2,1)S(1)}, u32[]{:S(2)}, u32[]{:S(2)}) collective-permute-start(bf16[1536,256]{1,0:T(8,128)(2,1)} %get-tuple-element.22), channel_id=1, source_target_pairs={{0,48},{48,0},{1,49},{49,1},{2,50},{50,2},{3,51},{51,3},{4,52},{52... | collective-permute-start | bytes 2359304 | tf_op jit(solution)/shard_map/ppermute | solution.py:237
  61.7 5.7 %copy-start.3 = (bf16[192,1024]{1,0:T(8,128)(2,1)}, bf16[192,1024]{1,0:T(8,128)(2,1)S(1)}, u32[]{:S(2)}) copy-start(bf16[192,1024]{1,0:T(8,128)(2,1)S(1)} %collective-permute-done.2.refs_3_) | copy-start | bytes 1179652
  61.9 5.6 %copy-start.4 = (bf16[192,1024]{1,0:T(8,128)(2,1)}, bf16[192,1024]{1,0:T(8,128)(2,1)S(1)}, u32[]{:S(2)}) copy-start(bf16[192,1024]{1,0:T(8,128)(2,1)S(1)} %collective-permute-done.1.refs_2_) | copy-start | bytes 1179652
  67.4 0.8 copy-start.5
  68.2 10.2 %copy-start.7 = (bf16[256,384]{1,0:T(8,128)(2,1)S(1)}, bf16[256,384]{1,0:T(8,128)(2,1)}, u32[]{:S(2)}) copy-start(bf16[256,384]{1,0:T(8,128)(2,1)} %get-tuple-element.25.ho) | copy-start | bytes 589828
  74.0 7.7 %collective-permute-start.7 = (bf16[1536,256]{1,0:T(8,128)(2,1)}, bf16[1536,256]{1,0:T(8,128)(2,1)S(1)}, u32[]{:S(2)}, u32[]{:S(2)}) collective-permute-start(bf16[1536,256]{1,0:T(8,128)(2,1)} %get-tuple-element.24), channel_id=1, source_target_pairs={{0,48},{48,0},{1,49},{49,1},{2,50},{50,2},{3,51},{51,3},{4,52},{52... | collective-permute-start | bytes 2359304 | tf_op jit(solution)/shard_map/ppermute | solution.py:237
  76.0 5.8 %collective-permute-start.8 = (bf16[256,768]{1,0:T(8,128)(2,1)}, bf16[256,768]{1,0:T(8,128)(2,1)S(1)}, u32[]{:S(2)}, u32[]{:S(2)}) collective-permute-start(bf16[256,768]{1,0:T(8,128)(2,1)} %get-tuple-element.16.both_ref.do), channel_id=1, source_target_pairs={{0,48},{48,0},{1,49},{49,1},{2,50},{50,2},{3,51},{51,3},{4,52},{52... | collective-permute-start | bytes 1179656 | tf_op jit(solution)/shard_map/ppermute | solution.py:237
  78.4 3.3 %collective-permute-start.9 = (bf16[256,384]{1,0:T(8,128)(2,1)S(1)}, bf16[256,384]{1,0:T(8,128)(2,1)S(1)}, u32[]{:S(2)}, u32[]{:S(2)}) collective-permute-start(bf16[256,384]{1,0:T(8,128)(2,1)S(1)} %copy-done.7), channel_id=1, source_target_pairs={{0,48},{48,0},{1,49},{49,1},{2,50},{50,2},{3,51},{51,3},{4,52},{52... | collective-permute-start | bytes 589832 | tf_op jit(solution)/shard_map/ppermute | solution.py:237
  81.7 0.7 copy-start.8
  81.7 1.0 copy-start.1
  81.7 1.1 copy-start.6
  81.8 1.3 copy-start.2
  95.5 14.1 %collective-permute-start.3 = (bf16[192,1024]{1,0:T(8,128)(2,1)}, bf16[192,1024]{1,0:T(8,128)(2,1)S(1)}, u32[]{:S(2)}, u32[]{:S(2)}) collective-permute-start(bf16[192,1024]{1,0:T(8,128)(2,1)} %get-tuple-element.18), channel_id=1, source_target_pairs={{0,1},{1,2},{2,3},{3,0},{4,5},{5,6},{6,7},{7,4},{8,9},{9,10},{10,1... | collective-permute-start | bytes 1179656 | tf_op jit(solution)/shard_map/ppermute | solution.py:240
  98.0 15.6 %collective-permute-start.4 = (bf16[192,1024]{1,0:T(8,128)(2,1)}, bf16[192,1024]{1,0:T(8,128)(2,1)S(1)}, u32[]{:S(2)}, u32[]{:S(2)}) collective-permute-start(bf16[192,1024]{1,0:T(8,128)(2,1)} %get-tuple-element.19), channel_id=1, source_target_pairs={{0,2},{1,3},{2,0},{3,1},{4,6},{5,7},{6,4},{7,5},{8,10},{9,11},{10,... | collective-permute-start | bytes 1179656 | tf_op jit(solution)/shard_map/ppermute | solution.py:240
  102.4 18.6 %collective-permute-start.5 = (bf16[192,1024]{1,0:T(8,128)(2,1)}, bf16[192,1024]{1,0:T(8,128)(2,1)S(1)}, u32[]{:S(2)}, u32[]{:S(2)}) collective-permute-start(bf16[192,1024]{1,0:T(8,128)(2,1)} %get-tuple-element.20), channel_id=1, source_target_pairs={{0,3},{1,0},{2,1},{3,2},{4,7},{5,4},{6,5},{7,6},{8,11},{9,8},{10,9... | collective-permute-start | bytes 1179656 | tf_op jit(solution)/shard_map/ppermute | solution.py:240
Sparse Core Ops, SparseCore 0:
  89.4 50.6 reduce-scatter.1

commit v2 on v1

--- a/solution.py
+++ b/solution.py
@@ -13,20 +13,20 @@
 TILE = 256
 F32 = jnp.float32
 BF16 = jnp.bfloat16
-LIMIT = 56 * 1024 * 1024
+MIB = 1024 * 1024
 NT = (((1,), (1,)), ((), ()))
 TN = (((0,), (0,)), ((), ()))
 VMEM = pl.BlockSpec(memory_space=pltpu.VMEM)
 SMEM = pl.BlockSpec(memory_space=pltpu.SMEM)
 
 
-def call(body, out_shape, in_specs, scratch=(), flops=0, moved=0, **more):
+def call(body, out_shape, in_specs, scratch=(), flops=0, moved=0, mib=16, **more):
     return pl.pallas_call(
         body,
         out_shape=out_shape,
         in_specs=in_specs,
         scratch_shapes=list(scratch),
-        compiler_params=pltpu.CompilerParams(vmem_limit_bytes=LIMIT),
+        compiler_params=pltpu.CompilerParams(vmem_limit_bytes=mib * MIB),
         cost_estimate=pl.CostEstimate(flops=flops, bytes_accessed=moved, transcendentals=0),
         **more,
     )
@@ -108,57 +108,73 @@
 
 
 def middle_body(cap, block, used, own, where_ref, *refs):
-    *bufs, wd_ref, act_ref, slope_ref, both_ref, own_ref, other_ref, dy, dyt = refs
+    *bufs, wd_ref, act_ref, slope_ref, ship_ref, own_ref, dy, dyt = refs
     core = where_ref[1]
     packed, part = bufs[0].shape
+    hid, width = wd_ref.shape
+    half = width // 2
+    rows = dy.shape[0]
     for p in range(PARTS):
         pick = picker(cap, block, used, packed, p)
         for j, buf in enumerate(bufs):
             dy[j * block : (j + 1) * block, p * part : (p + 1) * part] = jnp.dot(
                 pick, buf[...], preferred_element_type=F32
             ).astype(BF16)
-    hid = wd_ref.shape[0]
     d_hidden = lax.dot_general(dy[...], wd_ref[...], NT, preferred_element_type=F32)
-    both_ref[:, :hid] = (d_hidden * slope_ref[...]).astype(BF16)
-    both_ref[:, hid:] = (d_hidden * act_ref[...]).astype(BF16)
+    both = jnp.concatenate([d_hidden * slope_ref[...], d_hidden * act_ref[...]], axis=1).astype(BF16)
+    for k in range(2 * hid // rows):
+        ship_ref[half + k * rows : half + (k + 1) * rows, :] = both[:, k * rows : (k + 1) * rows]
     one = eye()
-    for t in range(dy.shape[1] // TILE):
+    for t in range(width // TILE):
         dyt[t * TILE : (t + 1) * TILE, :] = lax.dot_general(
             one, dy[:, t * TILE : (t + 1) * TILE], NT, preferred_element_type=F32
         ).astype(BF16)
-    split_halves(dyt, core, own_ref, other_ref, own)
-
-
-def back_body(cap, block, used, both_ref, wg_ref, wu_ref, *outs):
-    packed, part = outs[0].shape
+    split_halves(dyt, core, own_ref, ship_ref, own)
+
+
+def columns(ref, first, rows, n):
+    return [ref[first + k * rows : first + (k + 1) * rows, :] for k in range(n // rows)]
+
+
+def back_body(block, both_ref, wg_ref, wu_ref, *outs):
     hid = wg_ref.shape[0]
-    step = part // 2
-    picks = [picker(cap, block, used, packed, p) for p in range(PARTS)]
-    d_gate = both_ref[:, :hid]
-    d_up = both_ref[:, hid:]
-    for h in range(part // step):
-        pieces = []
+    rows = both_ref.shape[1]
+    both = jnp.concatenate(columns(both_ref, 0, rows, 2 * hid), axis=1)
+    dx = jnp.dot(both[:, :hid], wg_ref[...], preferred_element_type=F32)
+    dx = (dx + jnp.dot(both[:, hid:], wu_ref[...], preferred_element_type=F32)).astype(BF16)
+    for j, out in enumerate(outs):
+        out[...] = dx[j * block : (j + 1) * block, :]
+
+
+def merge_body(cap, used, *refs):
+    *bufs, out_ref, pack = refs
+    block, width = bufs[0].shape
+    depth = out_ref.shape[0]
+    part = width // PARTS
+    packed = depth * SLOT_ROWS
+    i = lax.broadcasted_iota(jnp.int32, (packed, block), 1)
+    q = lax.broadcasted_iota(jnp.int32, (packed, block), 0)
+    for h in range(part // TILE):
+        total = None
         for p in range(PARTS):
-            cols = slice(p * part + h * step, p * part + (h + 1) * step)
-            pieces.append(
-                (
-                    jnp.dot(d_gate, wg_ref[:, cols], preferred_element_type=F32)
-                    + jnp.dot(d_up, wu_ref[:, cols], preferred_element_type=F32)
-                ).astype(BF16)
-            )
-        for j, out in enumerate(outs):
-            total = None
-            for p in range(PARTS):
-                term = lax.dot_general(
-                    picks[p], pieces[p][j * block : (j + 1) * block, :], TN, preferred_element_type=F32
-                )
-                total = term if total is None else total + term
-            out[:, h * step : (h + 1) * step] = total.astype(BF16)
+            cols = slice(p * part + h * TILE, p * part + (h + 1) * TILE)
+            added = bufs[0][:, cols].astype(F32)
+            for buf in bufs[1:]:
+                added = added + buf[:, cols].astype(F32)
+            put = ((q == (i // cap) * SLOT_ROWS + p * cap + i % cap) & (i < used)).astype(BF16)
+            term = jnp.dot(put, added.astype(BF16), preferred_element_type=F32)
+            total = term if total is None else total + term
+        pack[:, h * TILE : (h + 1) * TILE] = total.astype(BF16)
+    for k in range(depth):
+        out_ref[k] = pack[k * SLOT_ROWS : (k + 1) * SLOT_ROWS, :]
 
 
 def terms_body(own, hid, xo, xp, yo, yp, do, dp, ho, hp, out):
-    both = jnp.dot(xo[...], do[...], preferred_element_type=F32)
-    both = both + jnp.dot(xp[...], dp[...], preferred_element_type=F32)
+    rows = xo.shape[1]
+    d_own = jnp.concatenate(columns(do, 0, rows, 2 * hid), axis=1)
+    d_pair = jnp.concatenate(columns(dp, 0, rows, 2 * hid), axis=1)
+    both = jnp.dot(xo[...], d_own, preferred_element_type=F32)
+    both = both + jnp.dot(xp[...], d_pair, preferred_element_type=F32)
     down = jnp.dot(yo[...], ho[...], preferred_element_type=F32)
     down = down + jnp.dot(yp[...], hp[...], preferred_element_type=F32)
     both = both.astype(BF16)
@@ -229,6 +245,7 @@
         ),
         [SMEM, VMEM, VMEM, VMEM],
         [pltpu.VMEM((rows, width), BF16), pltpu.VMEM((width, rows), BF16)],
+        mib=24,
         flops=2 * rows * width * (2 * hid + 2 * rows),
         moved=2 * width * (2 * hid + 2 * rows) + 10 * rows * hid,
     )(where, x_in, w_gate, w_up)
@@ -241,50 +258,63 @@
 
     x_pair = swap(x_other)
     hidden_pair = swap(hidden)
+    first, x_pair, hidden_pair = lax.optimization_barrier((first, x_pair, hidden_pair))
 
     mine = first.reshape(packed, part)
     bufs = [mine] + [shift(mine, -j) for j in range(1, n_x)]
-    both, y_own, y_other = call(
+    ship, y_own = call(
         functools.partial(middle_body, cap, block, used, own),
-        (shape((rows, 2 * hid), BF16), shape((half, rows), BF16), shape((half, rows), BF16)),
+        (shape((half + 2 * hid, rows), BF16), shape((half, rows), BF16)),
         [SMEM] + [VMEM] * (n_x + 3),
         [pltpu.VMEM((rows, width), BF16), pltpu.VMEM((width, rows), BF16)],
         flops=2 * rows * width * (hid + rows),
         moved=2 * width * (hid + 2 * rows) + 10 * rows * hid,
     )(where, *bufs, w_down, act, slope)
-    both_pair = swap(both)
-    y_pair = swap(y_other)
-
+    got = swap(ship)
+
+    step = 512
+    late = half // (2 * hid)
     back = call(
-        functools.partial(back_body, cap, block, used),
-        tuple(shape((packed, part), BF16) for _ in range(n_x)),
-        [VMEM] * 3,
-        flops=2 * rows * width * 3 * hid,
+        functools.partial(back_body, block),
+        tuple(shape((block, width), BF16) for _ in range(n_x)),
+        [pl.BlockSpec((2 * hid, rows), lambda g: (late, 0))] + [pl.BlockSpec((hid, step), lambda g: (0, g))] * 2,
+        flops=2 * rows * width * 2 * hid,
         moved=2 * width * (2 * hid + rows),
-    )(both, w_gate, w_up)
+        out_specs=tuple(pl.BlockSpec((block, step), lambda g: (0, g)) for _ in range(n_x)),
+        grid=(width // step,),
+    )(ship, w_gate, w_up)
+    got, back = lax.optimization_barrier((got, back))
 
     steps = n_y // 2
     per = n_y // steps
     feature = pl.BlockSpec((per * own, rows), lambda g: (g, 0))
-    whole = lambda n: pl.BlockSpec((rows, n), lambda g: (0, 0))
+    tail = pl.BlockSpec((2 * hid, rows), lambda g: (late, 0))
+    whole = pl.BlockSpec((rows, hid), lambda g: (0, 0))
     terms = call(
         functools.partial(terms_body, own, hid),
         shape((n_y, 3, own, hid), BF16),
-        [feature] * 4 + [whole(2 * hid)] * 2 + [whole(hid)] * 2,
+        [feature] * 4 + [tail] * 2 + [whole] * 2,
         flops=2 * 2 * rows * half * 3 * hid,
         moved=2 * half * (3 * hid + 4 * rows),
         out_specs=pl.BlockSpec((per, 3, own, hid), lambda g: (g, 0, 0, 0)),
         grid=(steps,),
-    )(x_own, x_pair, y_own, y_pair, both, both_pair, hidden, hidden_pair)
+    )(x_own, x_pair, y_own, got, ship, got, hidden, hidden_pair)
     shares = lax.psum_scatter(
         terms.reshape(n_y * 3 * own, hid), "y", scatter_dimension=0, tiled=True
     )
     weight_grads = shares.reshape(3, own, hid)
 
     arrived = [back[0]] + [shift(back[j], j) for j in range(1, n_x)]
-    added = sum(v.astype(F32) for v in arrived).astype(BF16)
+    added = call(
+        functools.partial(merge_body, cap, used),
+        shape((n_z, SLOT_ROWS, part), BF16),
+        [VMEM] * n_x,
+        [pltpu.VMEM((packed, part), BF16)],
+        flops=2 * packed * block * width,
+        moved=2 * n_x * block * width,
+    )(*arrived)
     returned = lax.all_to_all(
-        added.reshape(n_z, SLOT_ROWS, part), "z", split_axis=0, concat_axis=0, tiled=True
+        added, "z", split_axis=0, concat_axis=0, tiled=True
     )
     input_grad = call(
         functools.partial(final_body, cap),

time: 157 us -> 149 us (0.949)
  blocking collectives: 59.7 us -> 28.3 us
  starting transfers between devices: 26.4 us -> 40.5 us
  waiting for transfers between devices: 22.9 us -> 35.5 us
  Pallas kernels: 28.6 us -> 16.9 us
  local copies, waits for them, and re-layouts: 2.05 us -> 12.7 us
  other arithmetic: 1.87 us -> 0.08 us
    all_to_all x2 -> x1, blocking collectives: 59.7 us -> 28.3 us  [per_device(): lax.all_to_all(added, 'z', split_axis=0, concat_axis=0, tiled=True)]
    all_to_all x0 -> x1, starting transfers between devices: none -> 15.2 us  [per_device(): first = lax.all_to_all(sent, 'z', split_axis=0, concat_axis=0, tiled=True)]
    unnamed x18 -> x40, local copies, waits for them, and re-layouts: 2.05 us -> 12.7 us
    ppermute x6, waiting for transfers between devices: 21.5 us -> 32.1 us  [shift(): return lax.ppermute(v, 'x', [(i, (i + by) % n_x) for i in range(n_x)])]
    pallas_call x2 -> x3, Pallas kernels: 12.1 us -> 6.55 us  [the longest x1 3.12 us: per_device(): call(functools.partial(back_body, block), tuple((shape((block, width), BF...]
    pallas_call x1, Pallas kernels: 6.53 us -> 3.49 us  [per_device(): call(functools.partial(early_body, cap, n_x, block, own), (shape((half, r...]
    all_to_all x0 -> x1, waiting for transfers between devices: none -> 2.95 us  [per_device(): first = lax.all_to_all(sent, 'z', split_axis=0, concat_axis=0, tiled=True)]
    pallas_call x1, Pallas kernels: 6.19 us -> 3.92 us  [per_device(): call(functools.partial(terms_body, own, hid), shape((n_y, 3, own, hid), B...]
  transfers between devices with their start and end apart: 11 -> 11, of which waited for: 6 -> 6; matrix products, arithmetic and copies ran while one was open for 1% -> 0% of each run, Pallas kernels for 13% -> 6%
where the time goes in v2:
time: 149 us; the launch traced here: 148 us
  starting transfers between devices  40.5 us (27%)
  waiting for transfers between devices  35.5 us (24%)
  blocking collectives  28.3 us (19%)
  Pallas kernels  16.9 us (11%)
  between operations  14.3 us (10%)
  local copies, waits for them, and re-layouts  12.7 us (9%)
    ppermute x6, waiting for transfers between devices, shift(): return lax.ppermute(v, 'x', [(i, (i + by) % n_x) for i in range(n_x)])  32.1 us
    all_to_all x1, blocking collectives, per_device(): lax.all_to_all(added, 'z', split_axis=0, concat_axis=0, tiled=True)  28.3 us
    ppermute x6, starting transfers between devices, shift(): return lax.ppermute(v, 'x', [(i, (i + by) % n_x) for i in range(n_x)])  19 us
    all_to_all x1, starting transfers between devices, per_device(): first = lax.all_to_all(sent, 'z', split_axis=0, concat_axis=0, tiled=True)  15.2 us
    unnamed x40, local copies, waits for them, and re-layouts  12.7 us
    ppermute x3, starting transfers between devices, swap(): return lax.ppermute(v, 'c', [(i, (i + 1) % n_c) for i in range(n_c)])  6.37 us
    pallas_call x1, Pallas kernels, per_device(): call(functools.partial(terms_body, own, hid), shape((n_y, 3, own, hid), B...  3.92 us
    pallas_call x1, Pallas kernels, per_device(): call(functools.partial(early_body, cap, n_x, block, own), (shape((half, r...  3.49 us
  transfers between devices with their start and end apart: 11, of which 6 were waited for; matrix products, arithmetic and copies ran while one was open for 0% of the time, Pallas kernels for 6%

profile of v2, /device:TPU:6, one launch (start us, length us, event | category | flops | bytes accessed | tf_op | source)
XLA Modules:
  0.0 148.2 jit_solution(322388436096302059)
XLA Ops:
  7.2 0.9 copy-done.15
  8.7 0.7 copy-done.18
  9.4 1.5 %shard_map.86 = bf16[12,16,1024]{2,1,0:T(8,128)(2,1)} custom-call(s32[2,10]{1,0:T(2,128)S(1)} %bitcast.12, f32[2,10]{1,0:T(2,128)S(1)} %bitcast.14, bf16[10,3072]{1,0:T(8,128)(2,1)S(1)} %copy-done.15), custom_call_target="tpu_custom_call" | custom-call | bytes 500000 | tf_op jit(solution)/shard_map/pallas_call | solution.py:228
  10.9 15.2 %all-to-all-start = ((bf16[12,16,1024]{2,1,0:T(8,128)(2,1)}), bf16[12,16,1024]{2,1,0:T(8,128)(2,1)S(1)}, u32[]{:S(2)}, u32[]{:S(2)}) async-start(bf16[12,16,1024]{2,1,0:T(8,128)(2,1)} %shard_map.86), calls=%async_computation | async-start | bytes 786432 | tf_op jit(solution)/shard_map/all_to_all | solution.py:235
  26.2 1.7 %copy-done.1 = bf16[384,3072]{1,0:T(8,128)(2,1)S(1)} copy-done((bf16[384,3072]{1,0:T(8,128)(2,1)S(1)}, bf16[384,3072]{1,0:T(8,128)(2,1)}, u32[]{:S(2)}) %copy-start.1) | copy-done | bytes 2359320
  27.9 1.7 %copy-done.3 = bf16[384,3072]{1,0:T(8,128)(2,1)S(1)} copy-done((bf16[384,3072]{1,0:T(8,128)(2,1)S(1)}, bf16[384,3072]{1,0:T(8,128)(2,1)}, u32[]{:S(2)}) %copy-start.3) | copy-done | bytes 2359320
  29.6 1.4 copy-done.19
  30.9 3.5 %shard_map.87 = (bf16[1536,256]{1,0:T(8,128)(2,1)S(1)}, bf16[1536,256]{1,0:T(8,128)(2,1)S(1)}, f32[256,384]{1,0:T(8,128)S(1)}, f32[256,384]{1,0:T(8,128)S(1)}, bf16[256,384]{1,0:T(8,128)(2,1)S(1)}) custom-call(s32[2]{0:T(128)S(1)} %pad_add_fusion.where_ref, bf16[240,3072]{1,0:T(8,128)(2,1)S(1)} %bitcast.15, bf16[384,3072]{1,0:T(8,128)(2,1)S(1)} %copy-done.1, ...), custom_call_target="tpu_custom_call" | custom-call | flops 2013265920 | bytes 8847360 | tf_op jit(solution)/shard_map/pallas_call | solution.py:237
  34.4 0.8 copy-done.7
  35.2 0.7 copy-done.9
  36.0 1.9 %collective-permute-start = (bf16[1536,256]{1,0:T(8,128)(2,1)S(1)}, bf16[1536,256]{1,0:T(8,128)(2,1)S(1)}, u32[]{:S(2)}, u32[]{:S(2)}) collective-permute-start(bf16[1536,256]{1,0:T(8,128)(2,1)S(1)} %get-tuple-element.21), channel_id=1, source_target_pairs={{0,48},{48,0},{1,49},{49,1},{2,50},{50,2},{3,51},{51,3},{4,52},{52... | collective-permute-start | bytes 2359304 | tf_op jit(solution)/shard_map/ppermute | solution.py:254
  37.9 2.4 %collective-permute-start.1 = (bf16[256,384]{1,0:T(8,128)(2,1)S(1)}, bf16[256,384]{1,0:T(8,128)(2,1)S(1)}, u32[]{:S(2)}, u32[]{:S(2)}) collective-permute-start(bf16[256,384]{1,0:T(8,128)(2,1)S(1)} %get-tuple-element.22.ho), channel_id=1, source_target_pairs={{0,48},{48,0},{1,49},{49,1},{2,50},{50,2},{3,51},{51,3},{4,52},{52... | collective-permute-start | bytes 589832 | tf_op jit(solution)/shard_map/ppermute | solution.py:254
  42.0 0.9 copy-done.5
  42.9 3.0 %all-to-all-done = bf16[12,16,1024]{2,1,0:T(8,128)(2,1)S(1)} async-done(((bf16[12,16,1024]{2,1,0:T(8,128)(2,1)}), bf16[12,16,1024]{2,1,0:T(8,128)(2,1)S(1)}, u32[]{:S(2)}, u32[]{:S(2)}) %all-to-all-start) | async-done | bytes 393248 | tf_op jit(solution)/shard_map/all_to_all | solution.py:235
  45.9 2.7 %collective-permute-start.2 = (bf16[192,1024]{1,0:T(8,128)(2,1)S(1)}, bf16[192,1024]{1,0:T(8,128)(2,1)S(1)}, u32[]{:S(2)}, u32[]{:S(2)}) collective-permute-start(bf16[192,1024]{1,0:T(8,128)(2,1)S(1)} %bitcast.8), channel_id=1, source_target_pairs={{0,3},{1,0},{2,1},{3,2},{4,7},{5,4},{6,5},{7,6},{8,11},{9,8},{10,9... | collective-permute-start | bytes 1179656 | tf_op jit(solution)/shard_map/ppermute | solution.py:257
  48.6 3.0 %collective-permute-start.3 = (bf16[192,1024]{1,0:T(8,128)(2,1)S(1)}, bf16[192,1024]{1,0:T(8,128)(2,1)S(1)}, u32[]{:S(2)}, u32[]{:S(2)}) collective-permute-start(bf16[192,1024]{1,0:T(8,128)(2,1)S(1)} %bitcast.9), channel_id=1, source_target_pairs={{0,2},{1,3},{2,0},{3,1},{4,6},{5,7},{6,4},{7,5},{8,10},{9,11},{10,... | collective-permute-start | bytes 1179656 | tf_op jit(solution)/shard_map/ppermute | solution.py:257
  51.6 4.0 %collective-permute-start.4 = (bf16[192,1024]{1,0:T(8,128)(2,1)S(1)}, bf16[192,1024]{1,0:T(8,128)(2,1)S(1)}, u32[]{:S(2)}, u32[]{:S(2)}) collective-permute-start(bf16[192,1024]{1,0:T(8,128)(2,1)S(1)} %bitcast.10), channel_id=1, source_target_pairs={{0,1},{1,2},{2,3},{3,0},{4,5},{5,6},{6,7},{7,4},{8,9},{9,10},{10,1... | collective-permute-start | bytes 1179656 | tf_op jit(solution)/shard_map/ppermute | solution.py:257
  55.6 11.2 %collective-permute-done.2.refs_1_ = bf16[192,1024]{1,0:T(8,128)(2,1)S(1)} collective-permute-done((bf16[192,1024]{1,0:T(8,128)(2,1)S(1)}, bf16[192,1024]{1,0:T(8,128)(2,1)S(1)}, u32[]{:S(2)}, u32[]{:S(2)}) %collective-permute-start.2) | collective-permute-done | bytes 393248 | tf_op jit(solution)/shard_map/ppermute | solution.py:257
  66.9 2.5 %collective-permute-done.4.refs_3_ = bf16[192,1024]{1,0:T(8,128)(2,1)S(1)} collective-permute-done((bf16[192,1024]{1,0:T(8,128)(2,1)S(1)}, bf16[192,1024]{1,0:T(8,128)(2,1)S(1)}, u32[]{:S(2)}, u32[]{:S(2)}) %collective-permute-start.4) | collective-permute-done | bytes 393248 | tf_op jit(solution)/shard_map/ppermute | solution.py:257
  69.4 1.0 copy-done.8
  70.4 1.0 copy-done.10
  71.4 2.9 %shard_map.88 = (bf16[2304,256]{1,0:T(8,128)(2,1)S(1)}, bf16[1536,256]{1,0:T(8,128)(2,1)S(1)}) custom-call(s32[2]{0:T(128)S(1)} %pad_add_fusion.where_ref, bf16[192,1024]{1,0:T(8,128)(2,1)S(1)} %bitcast.11, bf16[192,1024]{1,0:T(8,128)(2,1)S(1)} %collective-permute-done.2.refs_1_, bf16[192,1024]{1,0:T(8,128)(2,1)S(1)} %collective-permute-done.3.refs_2_, ...), custom_call_target="tpu_custom_call" | custom-call | flops 1006632960 | bytes 6488064 | tf_op jit(solution)/shard_map/pallas_call | solution.py:265
  74.4 2.1 %collective-permute-start.5 = (bf16[2304,256]{1,0:T(8,128)(2,1)S(1)}, bf16[2304,256]{1,0:T(8,128)(2,1)S(1)}, u32[]{:S(2)}, u32[]{:S(2)}) collective-permute-start(bf16[2304,256]{1,0:T(8,128)(2,1)S(1)} %get-tuple-element.26.both_ref.do), channel_id=1, source_target_pairs={{0,48},{48,0},{1,49},{49,1},{2,50},{50,2},{3,51},{51,3},{4,52},{52... | collective-permute-start | bytes 3538952 | tf_op jit(solution)/shard_map/ppermute | solution.py:254
  76.5 3.1 %shard_map.89 = (bf16[64,3072]{1,0:T(8,128)(2,1)S(1)}, bf16[64,3072]{1,0:T(8,128)(2,1)S(1)}, bf16[64,3072]{1,0:T(8,128)(2,1)S(1)}, bf16[64,3072]{1,0:T(8,128)(2,1)S(1)}) custom-call(bf16[2304,256]{1,0:T(8,128)(2,1)S(1)} %get-tuple-element.26.both_ref.do, bf16[384,3072]{1,0:T(8,128)(2,1)S(1)} %copy-done.2, bf16[384,3072]{1,0:T(8,128)(2,1)S(1)} %copy-done.4), custom_call_target="tpu_custom_call" | custom-call | flops 1207959552 | bytes 6291456 | tf_op jit(solution)/shard_map/pallas_call | solution.py:277
  79.6 3.9 %shard_map.92 = bf16[8,3,192,384]{3,2,1,0:T(8,128)(2,1)} custom-call(bf16[1536,256]{1,0:T(8,128)(2,1)S(1)} %get-tuple-element.35.xo, bf16[1536,256]{1,0:T(8,128)(2,1)S(1)} %copy-done.6, bf16[1536,256]{1,0:T(8,128)(2,1)S(1)} %get-tuple-element.37.yo, bf16[2304,256]{1,0:T(8,128)(2,1)S(1)} %collective-permute-done.5.yp.dp, ...), custom_call_target="tpu_custom_call" | custom-call | flops 1811939328 | bytes 6684672 | tf_op jit(solution)/shard_map/pallas_call | solution.py:293
  83.6 4.5 %collective-permute-start.6 = (bf16[64,3072]{1,0:T(8,128)(2,1)S(1)}, bf16[64,3072]{1,0:T(8,128)(2,1)S(1)}, u32[]{:S(2)}, u32[]{:S(2)}) collective-permute-start(bf16[64,3072]{1,0:T(8,128)(2,1)S(1)} %get-tuple-element.32), channel_id=1, source_target_pairs={{0,1},{1,2},{2,3},{3,0},{4,5},{5,6},{6,7},{7,4},{8,9},{9,10},{10,1... | collective-permute-start | bytes 1179656 | tf_op jit(solution)/shard_map/ppermute | solution.py:257
  88.1 2.1 %collective-permute-start.7 = (bf16[64,3072]{1,0:T(8,128)(2,1)S(1)}, bf16[64,3072]{1,0:T(8,128)(2,1)S(1)}, u32[]{:S(2)}, u32[]{:S(2)}) collective-permute-start(bf16[64,3072]{1,0:T(8,128)(2,1)S(1)} %get-tuple-element.33), channel_id=1, source_target_pairs={{0,2},{1,3},{2,0},{3,1},{4,6},{5,7},{6,4},{7,5},{8,10},{9,11},{10,... | collective-permute-start | bytes 1179656 | tf_op jit(solution)/shard_map/ppermute | solution.py:257
  90.2 2.6 %collective-permute-start.8 = (bf16[64,3072]{1,0:T(8,128)(2,1)S(1)}, bf16[64,3072]{1,0:T(8,128)(2,1)S(1)}, u32[]{:S(2)}, u32[]{:S(2)}) collective-permute-start(bf16[64,3072]{1,0:T(8,128)(2,1)S(1)} %get-tuple-element.34), channel_id=1, source_target_pairs={{0,3},{1,0},{2,1},{3,2},{4,7},{5,4},{6,5},{7,6},{8,11},{9,8},{10,9... | collective-permute-start | bytes 1179656 | tf_op jit(solution)/shard_map/ppermute | solution.py:257
  92.8 12.8 %collective-permute-done.6.refs_1_ = bf16[64,3072]{1,0:T(8,128)(2,1)S(1)} collective-permute-done((bf16[64,3072]{1,0:T(8,128)(2,1)S(1)}, bf16[64,3072]{1,0:T(8,128)(2,1)S(1)}, u32[]{:S(2)}, u32[]{:S(2)}) %collective-permute-start.6) | collective-permute-done | bytes 393248 | tf_op jit(solution)/shard_map/ppermute | solution.py:257
  105.6 5.6 %collective-permute-done.8.refs_3_ = bf16[64,3072]{1,0:T(8,128)(2,1)S(1)} collective-permute-done((bf16[64,3072]{1,0:T(8,128)(2,1)S(1)}, bf16[64,3072]{1,0:T(8,128)(2,1)S(1)}, u32[]{:S(2)}, u32[]{:S(2)}) %collective-permute-start.8) | collective-permute-done | bytes 393248 | tf_op jit(solution)/shard_map/ppermute | solution.py:257
  111.7 28.3 %all_to_all.10.back_ref = bf16[12,16,1024]{2,1,0:T(8,128)(2,1)S(1)} all-to-all(bf16[12,16,1024]{2,1,0:T(8,128)(2,1)S(1)} %shard_map.90), channel_id=1, replica_groups=mesh['y'=8,'c'=2,'z'=12,'x'=4] {'z'}, dimensions={0} | all-to-all | bytes 786432 | tf_op jit(solution)/shard_map/all_to_all | solution.py:316
  140.0 1.4 shard_map.91
  (40 shorter events, 3.1 us)
Async XLA Ops:
  7.2 0.9 copy-start.15
  8.1 0.7 copy-start.16
  8.7 0.7 copy-start.18
  10.9 34.9 %all-to-all-start = ((bf16[12,16,1024]{2,1,0:T(8,128)(2,1)}), bf16[12,16,1024]{2,1,0:T(8,128)(2,1)S(1)}, u32[]{:S(2)}, u32[]{:S(2)}) async-start(bf16[12,16,1024]{2,1,0:T(8,128)(2,1)} %shard_map.86), calls=%async_computation | async-start | bytes 786432 | tf_op jit(solution)/shard_map/all_to_all | solution.py:235
  26.1 115.3 %reduce-scatter.2.cloned.1.call-start = ((), (), s32[]{:S(2)}) async-start(), calls=%async_computation.3 | async-start | bytes 3981312 | tf_op jit(solution)/shard_map/reduce_scatter | solution.py:302
  26.2 1.7 %copy-start.1 = (bf16[384,3072]{1,0:T(8,128)(2,1)S(1)}, bf16[384,3072]{1,0:T(8,128)(2,1)}, u32[]{:S(2)}) copy-start(bf16[384,3072]{1,0:T(8,128)(2,1)} %wg_ref.3) | copy-start | bytes 7077892
  27.9 1.7 %copy-start.3 = (bf16[384,3072]{1,0:T(8,128)(2,1)S(1)}, bf16[384,3072]{1,0:T(8,128)(2,1)}, u32[]{:S(2)}) copy-start(bf16[384,3072]{1,0:T(8,128)(2,1)} %wu_ref.3) | copy-start | bytes 7077892
  29.6 1.4 copy-start.19
  30.9 38.5 %copy-start = (bf16[384,3072]{1,0:T(8,128)(2,1)S(1)}, bf16[384,3072]{1,0:T(8,128)(2,1)}, u32[]{:S(2)}) copy-start(bf16[384,3072]{1,0:T(8,128)(2,1)} %refs_4_.1) | copy-start | bytes 7077892
  34.4 0.8 copy-start.7
  35.2 0.7 copy-start.9
  36.0 6.1 %collective-permute-start = (bf16[1536,256]{1,0:T(8,128)(2,1)S(1)}, bf16[1536,256]{1,0:T(8,128)(2,1)S(1)}, u32[]{:S(2)}, u32[]{:S(2)}) collective-permute-start(bf16[1536,256]{1,0:T(8,128)(2,1)S(1)} %get-tuple-element.21), channel_id=1, source_target_pairs={{0,48},{48,0},{1,49},{49,1},{2,50},{50,2},{3,51},{51,3},{4,52},{52... | collective-permute-start | bytes 2359304 | tf_op jit(solution)/shard_map/ppermute | solution.py:254
  37.9 3.5 %collective-permute-start.1 = (bf16[256,384]{1,0:T(8,128)(2,1)S(1)}, bf16[256,384]{1,0:T(8,128)(2,1)S(1)}, u32[]{:S(2)}, u32[]{:S(2)}) collective-permute-start(bf16[256,384]{1,0:T(8,128)(2,1)S(1)} %get-tuple-element.22.ho), channel_id=1, source_target_pairs={{0,48},{48,0},{1,49},{49,1},{2,50},{50,2},{3,51},{51,3},{4,52},{52... | collective-permute-start | bytes 589832 | tf_op jit(solution)/shard_map/ppermute | solution.py:254
  40.3 0.7 copy-start.11
  41.3 0.7 copy-start.13
  42.0 0.9 copy-start.5
  45.9 21.0 %collective-permute-start.2 = (bf16[192,1024]{1,0:T(8,128)(2,1)S(1)}, bf16[192,1024]{1,0:T(8,128)(2,1)S(1)}, u32[]{:S(2)}, u32[]{:S(2)}) collective-permute-start(bf16[192,1024]{1,0:T(8,128)(2,1)S(1)} %bitcast.8), channel_id=1, source_target_pairs={{0,3},{1,0},{2,1},{3,2},{4,7},{5,4},{6,5},{7,6},{8,11},{9,8},{10,9... | collective-permute-start | bytes 1179656 | tf_op jit(solution)/shard_map/ppermute | solution.py:257
  48.6 18.3 %collective-permute-start.3 = (bf16[192,1024]{1,0:T(8,128)(2,1)S(1)}, bf16[192,1024]{1,0:T(8,128)(2,1)S(1)}, u32[]{:S(2)}, u32[]{:S(2)}) collective-permute-start(bf16[192,1024]{1,0:T(8,128)(2,1)S(1)} %bitcast.9), channel_id=1, source_target_pairs={{0,2},{1,3},{2,0},{3,1},{4,6},{5,7},{6,4},{7,5},{8,10},{9,11},{10,... | collective-permute-start | bytes 1179656 | tf_op jit(solution)/shard_map/ppermute | solution.py:257
  51.6 17.8 %collective-permute-start.4 = (bf16[192,1024]{1,0:T(8,128)(2,1)S(1)}, bf16[192,1024]{1,0:T(8,128)(2,1)S(1)}, u32[]{:S(2)}, u32[]{:S(2)}) collective-permute-start(bf16[192,1024]{1,0:T(8,128)(2,1)S(1)} %bitcast.10), channel_id=1, source_target_pairs={{0,1},{1,2},{2,3},{3,0},{4,5},{5,6},{6,7},{7,4},{8,9},{9,10},{10,1... | collective-permute-start | bytes 1179656 | tf_op jit(solution)/shard_map/ppermute | solution.py:257
  69.4 1.0 copy-start.8
  70.4 1.0 copy-start.10
  71.4 5.0 %copy-start.2 = (bf16[384,3072]{1,0:T(8,128)(2,1)S(1)}, bf16[384,3072]{1,0:T(8,128)(2,1)}, u32[]{:S(2)}) copy-start(bf16[384,3072]{1,0:T(8,128)(2,1)} %wg_ref.3) | copy-start | bytes 7077892
  71.4 5.0 %copy-start.4 = (bf16[384,3072]{1,0:T(8,128)(2,1)S(1)}, bf16[384,3072]{1,0:T(8,128)(2,1)}, u32[]{:S(2)}) copy-start(bf16[384,3072]{1,0:T(8,128)(2,1)} %wu_ref.3) | copy-start | bytes 7077892
  74.4 5.3 %copy-start.6 = (bf16[1536,256]{1,0:T(8,128)(2,1)S(1)}, bf16[1536,256]{1,0:T(8,128)(2,1)}, u32[]{:S(2)}) copy-start(bf16[1536,256]{1,0:T(8,128)(2,1)} %copy-done.5) | copy-start | bytes 2359300
  74.4 5.3 %copy-start.12 = (bf16[256,384]{1,0:T(8,128)(2,1)S(1)}, bf16[256,384]{1,0:T(8,128)(2,1)}, u32[]{:S(2)}) copy-start(bf16[256,384]{1,0:T(8,128)(2,1)} %copy-done.11) | copy-start | bytes 589828
  74.4 5.3 %copy-start.14 = (bf16[256,384]{1,0:T(8,128)(2,1)S(1)}, bf16[256,384]{1,0:T(8,128)(2,1)}, u32[]{:S(2)}) copy-start(bf16[256,384]{1,0:T(8,128)(2,1)} %copy-done.13) | copy-start | bytes 589828
  74.4 5.2 %collective-permute-start.5 = (bf16[2304,256]{1,0:T(8,128)(2,1)S(1)}, bf16[2304,256]{1,0:T(8,128)(2,1)S(1)}, u32[]{:S(2)}, u32[]{:S(2)}) collective-permute-start(bf16[2304,256]{1,0:T(8,128)(2,1)S(1)} %get-tuple-element.26.both_ref.do), channel_id=1, source_target_pairs={{0,48},{48,0},{1,49},{49,1},{2,50},{50,2},{3,51},{51,3},{4,52},{52... | collective-permute-start | bytes 3538952 | tf_op jit(solution)/shard_map/ppermute | solution.py:254
  83.6 56.4 %copy-start.17 = (s32[10,2]{0,1:T(2,128)S(1)}, s32[10,2]{0,1:T(2,128)}, u32[]{:S(2)}) copy-start(s32[10,2]{0,1:T(2,128)} %param.8) | copy-start | bytes 244
  83.6 22.0 %collective-permute-start.6 = (bf16[64,3072]{1,0:T(8,128)(2,1)S(1)}, bf16[64,3072]{1,0:T(8,128)(2,1)S(1)}, u32[]{:S(2)}, u32[]{:S(2)}) collective-permute-start(bf16[64,3072]{1,0:T(8,128)(2,1)S(1)} %get-tuple-element.32), channel_id=1, source_target_pairs={{0,1},{1,2},{2,3},{3,0},{4,5},{5,6},{6,7},{7,4},{8,9},{9,10},{10,1... | collective-permute-start | bytes 1179656 | tf_op jit(solution)/shard_map/ppermute | solution.py:257
  88.1 17.5 %collective-permute-start.7 = (bf16[64,3072]{1,0:T(8,128)(2,1)S(1)}, bf16[64,3072]{1,0:T(8,128)(2,1)S(1)}, u32[]{:S(2)}, u32[]{:S(2)}) collective-permute-start(bf16[64,3072]{1,0:T(8,128)(2,1)S(1)} %get-tuple-element.33), channel_id=1, source_target_pairs={{0,2},{1,3},{2,0},{3,1},{4,6},{5,7},{6,4},{7,5},{8,10},{9,11},{10,... | collective-permute-start | bytes 1179656 | tf_op jit(solution)/shard_map/ppermute | solution.py:257
  90.2 21.0 %collective-permute-start.8 = (bf16[64,3072]{1,0:T(8,128)(2,1)S(1)}, bf16[64,3072]{1,0:T(8,128)(2,1)S(1)}, u32[]{:S(2)}, u32[]{:S(2)}) collective-permute-start(bf16[64,3072]{1,0:T(8,128)(2,1)S(1)} %get-tuple-element.34), channel_id=1, source_target_pairs={{0,3},{1,0},{2,1},{3,2},{4,7},{5,4},{6,5},{7,6},{8,11},{9,8},{10,9... | collective-permute-start | bytes 1179656 | tf_op jit(solution)/shard_map/ppermute | solution.py:257
Sparse Core Ops, SparseCore 0:
  83.7 54.2 reduce-scatter.1

commit v3 on v2

--- a/solution.py
+++ b/solution.py
@@ -18,6 +18,7 @@
 TN = (((0,), (0,)), ((), ()))
 VMEM = pl.BlockSpec(memory_space=pltpu.VMEM)
 SMEM = pl.BlockSpec(memory_space=pltpu.SMEM)
+HBM = pl.BlockSpec(memory_space=pltpu.HBM)
 
 
 def call(body, out_shape, in_specs, scratch=(), flops=0, moved=0, mib=16, **more):
@@ -76,7 +77,16 @@
         other_ref[g * own : (g + 1) * own, :] = full[pl.ds(theirs, own), :]
 
 
-def early_body(cap, n_x, block, own, where_ref, x_ref, wg_ref, wu_ref, own_ref, other_ref, act_ref, slope_ref, hidden_ref, xp, xt):
+def start_all(pairs, sems, first=0):
+    copies = [pltpu.make_async_copy(a, b, sems.at[first + n]) for n, (a, b) in enumerate(pairs)]
+    for copy in copies:
+        copy.start()
+    return copies
+
+
+def early_body(cap, n_x, block, own, where_ref, x_at, wg_at, wu_at, own_at, other_at, act_at, slope_at, hidden_at, *scratch):
+    xp, xt, x_ref, wg_ref, wu_ref, own_ref, other_ref, act_ref, slope_ref, hidden_ref, sems = scratch
+    fetches = start_all(((x_at, x_ref), (wg_at, wg_ref), (wu_at, wu_ref)), sems)
     rows, width = xp.shape
     used = x_ref.shape[0] // n_x
     at = where_ref[0]
@@ -87,18 +97,25 @@
     source = (at + r // block) % n_x
     order = ((q == ((i // cap) * n_x + source) * cap + i % cap) & (i < used)).astype(BF16)
     one = eye()
+    fetches[0].wait()
     for t in range(width // TILE):
         piece = jnp.dot(order, x_ref[:, t * TILE : (t + 1) * TILE], preferred_element_type=F32).astype(BF16)
         xp[:, t * TILE : (t + 1) * TILE] = piece
         xt[t * TILE : (t + 1) * TILE, :] = lax.dot_general(one, piece, NT, preferred_element_type=F32).astype(BF16)
     split_halves(xt, core, own_ref, other_ref, own)
+    stores = start_all(((other_ref, other_at), (own_ref, own_at)), sems, 3)
+    fetches[1].wait()
     gate = lax.dot_general(xp[...], wg_ref[...], NT, preferred_element_type=F32)
+    fetches[2].wait()
     upper = lax.dot_general(xp[...], wu_ref[...], NT, preferred_element_type=F32)
     sigma = jax.nn.sigmoid(gate)
     act = gate * sigma
     act_ref[...] = act
     slope_ref[...] = upper * sigma * (1.0 + gate * (1.0 - sigma))
     hidden_ref[...] = (act * upper).astype(BF16)
+    stores += start_all(((hidden_ref, hidden_at), (act_ref, act_at), (slope_ref, slope_at)), sems, 5)
+    for store in stores:
+        store.wait()
 
 
 def picker(cap, block, used, packed, part):
@@ -108,7 +125,8 @@
 
 
 def middle_body(cap, block, used, own, where_ref, *refs):
-    *bufs, wd_ref, act_ref, slope_ref, ship_ref, own_ref, dy, dyt = refs
+    *bufs, wd_at, act_at, slope_at, ship_ref, own_ref, dy, dyt, wd_ref, act_ref, slope_ref, arrived = refs
+    fetches = start_all(((wd_at, wd_ref), (act_at, act_ref), (slope_at, slope_ref)), arrived)
     core = where_ref[1]
     packed, part = bufs[0].shape
     hid, width = wd_ref.shape
@@ -120,7 +138,10 @@
             dy[j * block : (j + 1) * block, p * part : (p + 1) * part] = jnp.dot(
                 pick, buf[...], preferred_element_type=F32
             ).astype(BF16)
+    fetches[0].wait()
     d_hidden = lax.dot_general(dy[...], wd_ref[...], NT, preferred_element_type=F32)
+    fetches[1].wait()
+    fetches[2].wait()
     both = jnp.concatenate([d_hidden * slope_ref[...], d_hidden * act_ref[...]], axis=1).astype(BF16)
     for k in range(2 * hid // rows):
         ship_ref[half + k * rows : half + (k + 1) * rows, :] = both[:, k * rows : (k + 1) * rows]
@@ -231,6 +252,7 @@
         [SMEM, SMEM, VMEM],
         [pltpu.VMEM(((EXPERTS + 1) * SLOT_ROWS, part), F32)],
         moved=500_000,
+        mib=56,
     )(routes_t, probs_t, d_out)
     first = lax.all_to_all(sent, "z", split_axis=0, concat_axis=0, tiled=True)
 
@@ -243,9 +265,22 @@
             shape((rows, hid), F32),
             shape((rows, hid), BF16),
         ),
-        [SMEM, VMEM, VMEM, VMEM],
-        [pltpu.VMEM((rows, width), BF16), pltpu.VMEM((width, rows), BF16)],
-        mib=24,
+        [SMEM, HBM, HBM, HBM],
+        [
+            pltpu.VMEM((rows, width), BF16),
+            pltpu.VMEM((width, rows), BF16),
+            pltpu.VMEM(x_in.shape, BF16),
+            pltpu.VMEM(w_gate.shape, BF16),
+            pltpu.VMEM(w_up.shape, BF16),
+            pltpu.VMEM((half, rows), BF16),
+            pltpu.VMEM((half, rows), BF16),
+            pltpu.VMEM((rows, hid), F32),
+            pltpu.VMEM((rows, hid), F32),
+            pltpu.VMEM((rows, hid), BF16),
+            pltpu.SemaphoreType.DMA((8,)),
+        ],
+        mib=60,
+        out_specs=(HBM,) * 5,
         flops=2 * rows * width * (2 * hid + 2 * rows),
         moved=2 * width * (2 * hid + 2 * rows) + 10 * rows * hid,
     )(where, x_in, w_gate, w_up)
@@ -258,15 +293,23 @@
 
     x_pair = swap(x_other)
     hidden_pair = swap(hidden)
+
     first, x_pair, hidden_pair = lax.optimization_barrier((first, x_pair, hidden_pair))
-
     mine = first.reshape(packed, part)
     bufs = [mine] + [shift(mine, -j) for j in range(1, n_x)]
     ship, y_own = call(
         functools.partial(middle_body, cap, block, used, own),
         (shape((half + 2 * hid, rows), BF16), shape((half, rows), BF16)),
-        [SMEM] + [VMEM] * (n_x + 3),
-        [pltpu.VMEM((rows, width), BF16), pltpu.VMEM((width, rows), BF16)],
+        [SMEM] + [VMEM] * n_x + [HBM] * 3,
+        [
+            pltpu.VMEM((rows, width), BF16),
+            pltpu.VMEM((width, rows), BF16),
+            pltpu.VMEM(w_down.shape, BF16),
+            pltpu.VMEM((rows, hid), F32),
+            pltpu.VMEM((rows, hid), F32),
+            pltpu.SemaphoreType.DMA((3,)),
+        ],
+        mib=16,
         flops=2 * rows * width * (hid + rows),
         moved=2 * width * (hid + 2 * rows) + 10 * rows * hid,
     )(where, *bufs, w_down, act, slope)

time: 149 us -> 145 us (0.973)
  local copies, waits for them, and re-layouts: 12.7 us -> 2.71 us
  Pallas kernels: 16.9 us -> 21.2 us
  waiting for transfers between devices: 35.5 us -> 39.7 us
  blocking collectives: 28.3 us -> 24.9 us
    unnamed x40 -> x22, local copies, waits for them, and re-layouts: 12.7 us -> 2.71 us
    all_to_all x1, waiting for transfers between devices: 2.95 us -> 6.28 us  [per_device(): first = lax.all_to_all(sent, 'z', split_axis=0, concat_axis=0, tiled=True)]
    all_to_all x1, blocking collectives: 28.3 us -> 24.9 us  [per_device(): lax.all_to_all(added, 'z', split_axis=0, concat_axis=0, tiled=True)]
    pallas_call x1, Pallas kernels: 3.49 us -> 6.47 us  [per_device(): call(functools.partial(early_body, cap, n_x, block, own), (shape((half, r...]
  transfers between devices with their start and end apart: 11 -> 11, of which waited for: 6 -> 6; matrix products, arithmetic and copies ran while one was open for 0% -> 0% of each run, Pallas kernels for 6% -> 8%
where the time goes in v3:
time: 145 us; the launch traced here: 144 us
  starting transfers between devices  40.6 us (28%)
  waiting for transfers between devices  39.7 us (27%)
  blocking collectives  24.9 us (17%)
  Pallas kernels  21.2 us (15%)
  between operations  14.2 us (10%)
  local copies, waits for them, and re-layouts  2.71 us (2%)
    ppermute x6, waiting for transfers between devices, shift(): return lax.ppermute(v, 'x', [(i, (i + by) % n_x) for i in range(n_x)])  32.1 us
    all_to_all x1, blocking collectives, per_device(): lax.all_to_all(added, 'z', split_axis=0, concat_axis=0, tiled=True)  24.9 us
    ppermute x6, starting transfers between devices, shift(): return lax.ppermute(v, 'x', [(i, (i + by) % n_x) for i in range(n_x)])  19 us
    all_to_all x1, starting transfers between devices, per_device(): first = lax.all_to_all(sent, 'z', split_axis=0, concat_axis=0, tiled=True)  15.2 us
    pallas_call x1, Pallas kernels, per_device(): call(functools.partial(early_body, cap, n_x, block, own), (shape((half, r...  6.47 us
    ppermute x3, starting transfers between devices, swap(): return lax.ppermute(v, 'c', [(i, (i + 1) % n_c) for i in range(n_c)])  6.38 us
    all_to_all x1, waiting for transfers between devices, per_device(): first = lax.all_to_all(sent, 'z', split_axis=0, concat_axis=0, tiled=True)  6.28 us
    pallas_call x1, Pallas kernels, per_device(): call(functools.partial(terms_body, own, hid), shape((n_y, 3, own, hid), B...  3.95 us
  transfers between devices with their start and end apart: 11, of which 6 were waited for; matrix products, arithmetic and copies ran while one was open for 0% of the time, Pallas kernels for 8%

profile of v3, /device:TPU:6, one launch (start us, length us, event | category | flops | bytes accessed | tf_op | source)
XLA Modules:
  0.0 144.0 jit_solution(5374349771476680048)
XLA Ops:
  7.2 1.9 %shard_map.86 = bf16[12,16,1024]{2,1,0:T(8,128)(2,1)} custom-call(s32[2,10]{1,0:T(2,128)} %bitcast.12, f32[2,10]{1,0:T(2,128)} %bitcast.14, bf16[10,3072]{1,0:T(8,128)(2,1)} %d_ref.1), custom_call_target="tpu_custom_call" | custom-call | bytes 500000 | tf_op jit(solution)/shard_map/pallas_call | solution.py:249
  9.0 15.2 %all-to-all-start = ((bf16[12,16,1024]{2,1,0:T(8,128)(2,1)}), bf16[12,16,1024]{2,1,0:T(8,128)(2,1)S(1)}, u32[]{:S(2)}, u32[]{:S(2)}) async-start(bf16[12,16,1024]{2,1,0:T(8,128)(2,1)} %shard_map.86), calls=%async_computation | async-start | bytes 786432 | tf_op jit(solution)/shard_map/all_to_all | solution.py:257
  24.2 0.0 reduce-scatter.2.cloned.1.call-start
  24.3 0.7 pad_add_fusion.where_ref
  24.9 6.5 %shard_map.87 = (bf16[1536,256]{1,0:T(8,128)(2,1)}, bf16[1536,256]{1,0:T(8,128)(2,1)}, f32[256,384]{1,0:T(8,128)}, f32[256,384]{1,0:T(8,128)}, bf16[256,384]{1,0:T(8,128)(2,1)}) custom-call(s32[2]{0:T(128)} %pad_add_fusion.where_ref, bf16[240,3072]{1,0:T(8,128)(2,1)} %bitcast.15, bf16[384,3072]{1,0:T(8,128)(2,1)} %wg_ref.1, bf16[384,3072]{1,0:T(8,128)(2,1)} %wu_ref.1), custom_call_target="tpu_custom_call" | custom-call | flops 2013265920 | bytes 8847360 | tf_op jit(solution)/shard_map/pallas_call | solution.py:259
  31.4 1.9 %collective-permute-start = (bf16[1536,256]{1,0:T(8,128)(2,1)}, bf16[1536,256]{1,0:T(8,128)(2,1)S(1)}, u32[]{:S(2)}, u32[]{:S(2)}) collective-permute-start(bf16[1536,256]{1,0:T(8,128)(2,1)} %get-tuple-element.21), channel_id=1, source_target_pairs={{0,48},{48,0},{1,49},{49,1},{2,50},{50,2},{3,51},{51,3},{4,52},{52... | collective-permute-start | bytes 2359304 | tf_op jit(solution)/shard_map/ppermute | solution.py:289
  33.3 2.4 %collective-permute-start.1 = (bf16[256,384]{1,0:T(8,128)(2,1)}, bf16[256,384]{1,0:T(8,128)(2,1)S(1)}, u32[]{:S(2)}, u32[]{:S(2)}) collective-permute-start(bf16[256,384]{1,0:T(8,128)(2,1)} %get-tuple-element.22.ho), channel_id=1, source_target_pairs={{0,48},{48,0},{1,49},{49,1},{2,50},{50,2},{3,51},{51,3},{4,52},{52... | collective-permute-start | bytes 589832 | tf_op jit(solution)/shard_map/ppermute | solution.py:289
  35.7 1.3 collective-permute-done.1.hp
  37.0 0.7 copy-done.7
  37.7 0.0 collective-permute-done.xp
  37.7 6.3 %all-to-all-done = bf16[12,16,1024]{2,1,0:T(8,128)(2,1)S(1)} async-done(((bf16[12,16,1024]{2,1,0:T(8,128)(2,1)}), bf16[12,16,1024]{2,1,0:T(8,128)(2,1)S(1)}, u32[]{:S(2)}, u32[]{:S(2)}) %all-to-all-start) | async-done | bytes 393248 | tf_op jit(solution)/shard_map/all_to_all | solution.py:257
  44.0 2.7 %collective-permute-start.2 = (bf16[192,1024]{1,0:T(8,128)(2,1)S(1)}, bf16[192,1024]{1,0:T(8,128)(2,1)S(1)}, u32[]{:S(2)}, u32[]{:S(2)}) collective-permute-start(bf16[192,1024]{1,0:T(8,128)(2,1)S(1)} %bitcast.8), channel_id=1, source_target_pairs={{0,3},{1,0},{2,1},{3,2},{4,7},{5,4},{6,5},{7,6},{8,11},{9,8},{10,9... | collective-permute-start | bytes 1179656 | tf_op jit(solution)/shard_map/ppermute | solution.py:292
  46.7 3.0 %collective-permute-start.3 = (bf16[192,1024]{1,0:T(8,128)(2,1)S(1)}, bf16[192,1024]{1,0:T(8,128)(2,1)S(1)}, u32[]{:S(2)}, u32[]{:S(2)}) collective-permute-start(bf16[192,1024]{1,0:T(8,128)(2,1)S(1)} %bitcast.9), channel_id=1, source_target_pairs={{0,2},{1,3},{2,0},{3,1},{4,6},{5,7},{6,4},{7,5},{8,10},{9,11},{10,... | collective-permute-start | bytes 1179656 | tf_op jit(solution)/shard_map/ppermute | solution.py:292
  49.7 4.0 %collective-permute-start.4 = (bf16[192,1024]{1,0:T(8,128)(2,1)S(1)}, bf16[192,1024]{1,0:T(8,128)(2,1)S(1)}, u32[]{:S(2)}, u32[]{:S(2)}) collective-permute-start(bf16[192,1024]{1,0:T(8,128)(2,1)S(1)} %bitcast.10), channel_id=1, source_target_pairs={{0,1},{1,2},{2,3},{3,0},{4,5},{5,6},{6,7},{7,4},{8,9},{9,10},{10,1... | collective-permute-start | bytes 1179656 | tf_op jit(solution)/shard_map/ppermute | solution.py:292
  53.7 11.2 %collective-permute-done.2.refs_1_ = bf16[192,1024]{1,0:T(8,128)(2,1)S(1)} collective-permute-done((bf16[192,1024]{1,0:T(8,128)(2,1)S(1)}, bf16[192,1024]{1,0:T(8,128)(2,1)S(1)}, u32[]{:S(2)}, u32[]{:S(2)}) %collective-permute-start.2) | collective-permute-done | bytes 393248 | tf_op jit(solution)/shard_map/ppermute | solution.py:292
  65.0 0.0 collective-permute-done.3.refs_2_
  65.0 2.5 %collective-permute-done.4.refs_3_ = bf16[192,1024]{1,0:T(8,128)(2,1)S(1)} collective-permute-done((bf16[192,1024]{1,0:T(8,128)(2,1)S(1)}, bf16[192,1024]{1,0:T(8,128)(2,1)S(1)}, u32[]{:S(2)}, u32[]{:S(2)}) %collective-permute-start.4) | collective-permute-done | bytes 393248 | tf_op jit(solution)/shard_map/ppermute | solution.py:292
  67.5 1.0 copy-done.4
  68.5 1.0 copy-done.5
  69.5 3.9 %shard_map.88 = (bf16[2304,256]{1,0:T(8,128)(2,1)S(1)}, bf16[1536,256]{1,0:T(8,128)(2,1)S(1)}) custom-call(s32[2]{0:T(128)S(1)} %copy-done.10, bf16[192,1024]{1,0:T(8,128)(2,1)S(1)} %bitcast.11, bf16[192,1024]{1,0:T(8,128)(2,1)S(1)} %collective-permute-done.2.refs_1_, bf16[192,1024]{1,0:T(8,128)(2,1)S(1)} %collective-permute-done.3.refs_2_, ...), custom_call_target="tpu_custom_call" | custom-call | flops 1006632960 | bytes 6488064 | tf_op jit(solution)/shard_map/pallas_call | solution.py:300
  73.5 2.1 %collective-permute-start.5 = (bf16[2304,256]{1,0:T(8,128)(2,1)S(1)}, bf16[2304,256]{1,0:T(8,128)(2,1)S(1)}, u32[]{:S(2)}, u32[]{:S(2)}) collective-permute-start(bf16[2304,256]{1,0:T(8,128)(2,1)S(1)} %get-tuple-element.26.both_ref.do), channel_id=1, source_target_pairs={{0,48},{48,0},{1,49},{49,1},{2,50},{50,2},{3,51},{51,3},{4,52},{52... | collective-permute-start | bytes 3538952 | tf_op jit(solution)/shard_map/ppermute | solution.py:289
  75.6 3.1 %shard_map.89 = (bf16[64,3072]{1,0:T(8,128)(2,1)S(1)}, bf16[64,3072]{1,0:T(8,128)(2,1)S(1)}, bf16[64,3072]{1,0:T(8,128)(2,1)S(1)}, bf16[64,3072]{1,0:T(8,128)(2,1)S(1)}) custom-call(bf16[2304,256]{1,0:T(8,128)(2,1)S(1)} %get-tuple-element.26.both_ref.do, bf16[384,3072]{1,0:T(8,128)(2,1)S(1)} %copy-done.1, bf16[384,3072]{1,0:T(8,128)(2,1)S(1)} %copy-done.2), custom_call_target="tpu_custom_call" | custom-call | flops 1207959552 | bytes 6291456 | tf_op jit(solution)/shard_map/pallas_call | solution.py:320
  78.7 3.9 %shard_map.92 = bf16[8,3,192,384]{3,2,1,0:T(8,128)(2,1)} custom-call(bf16[1536,256]{1,0:T(8,128)(2,1)S(1)} %copy-done.3, bf16[1536,256]{1,0:T(8,128)(2,1)S(1)} %collective-permute-done.xp, bf16[1536,256]{1,0:T(8,128)(2,1)S(1)} %get-tuple-element.37.yo, bf16[2304,256]{1,0:T(8,128)(2,1)S(1)} %collective-permute-done.5.yp.dp, ...), custom_call_target="tpu_custom_call" | custom-call | flops 1811939328 | bytes 6684672 | tf_op jit(solution)/shard_map/pallas_call | solution.py:336
  82.7 0.0 reduce-scatter.2.cloned.1.call-update
  82.7 4.5 %collective-permute-start.6 = (bf16[64,3072]{1,0:T(8,128)(2,1)S(1)}, bf16[64,3072]{1,0:T(8,128)(2,1)S(1)}, u32[]{:S(2)}, u32[]{:S(2)}) collective-permute-start(bf16[64,3072]{1,0:T(8,128)(2,1)S(1)} %get-tuple-element.32), channel_id=1, source_target_pairs={{0,1},{1,2},{2,3},{3,0},{4,5},{5,6},{6,7},{7,4},{8,9},{9,10},{10,1... | collective-permute-start | bytes 1179656 | tf_op jit(solution)/shard_map/ppermute | solution.py:292
  87.3 2.1 %collective-permute-start.7 = (bf16[64,3072]{1,0:T(8,128)(2,1)S(1)}, bf16[64,3072]{1,0:T(8,128)(2,1)S(1)}, u32[]{:S(2)}, u32[]{:S(2)}) collective-permute-start(bf16[64,3072]{1,0:T(8,128)(2,1)S(1)} %get-tuple-element.33), channel_id=1, source_target_pairs={{0,2},{1,3},{2,0},{3,1},{4,6},{5,7},{6,4},{7,5},{8,10},{9,11},{10,... | collective-permute-start | bytes 1179656 | tf_op jit(solution)/shard_map/ppermute | solution.py:292
  89.4 2.6 %collective-permute-start.8 = (bf16[64,3072]{1,0:T(8,128)(2,1)S(1)}, bf16[64,3072]{1,0:T(8,128)(2,1)S(1)}, u32[]{:S(2)}, u32[]{:S(2)}) collective-permute-start(bf16[64,3072]{1,0:T(8,128)(2,1)S(1)} %get-tuple-element.34), channel_id=1, source_target_pairs={{0,3},{1,0},{2,1},{3,2},{4,7},{5,4},{6,5},{7,6},{8,11},{9,8},{10,9... | collective-permute-start | bytes 1179656 | tf_op jit(solution)/shard_map/ppermute | solution.py:292
  92.0 12.8 %collective-permute-done.6.refs_1_ = bf16[64,3072]{1,0:T(8,128)(2,1)S(1)} collective-permute-done((bf16[64,3072]{1,0:T(8,128)(2,1)S(1)}, bf16[64,3072]{1,0:T(8,128)(2,1)S(1)}, u32[]{:S(2)}, u32[]{:S(2)}) %collective-permute-start.6) | collective-permute-done | bytes 393248 | tf_op jit(solution)/shard_map/ppermute | solution.py:292
  104.7 5.6 %collective-permute-done.8.refs_3_ = bf16[64,3072]{1,0:T(8,128)(2,1)S(1)} collective-permute-done((bf16[64,3072]{1,0:T(8,128)(2,1)S(1)}, bf16[64,3072]{1,0:T(8,128)(2,1)S(1)}, u32[]{:S(2)}, u32[]{:S(2)}) %collective-permute-start.8) | collective-permute-done | bytes 393248 | tf_op jit(solution)/shard_map/ppermute | solution.py:292
  110.3 0.5 shard_map.90
  110.8 24.9 %all_to_all.10.back_ref = bf16[12,16,1024]{2,1,0:T(8,128)(2,1)S(1)} all-to-all(bf16[12,16,1024]{2,1,0:T(8,128)(2,1)S(1)} %shard_map.90), channel_id=1, replica_groups=mesh['y'=8,'c'=2,'z'=12,'x'=4] {'z'}, dimensions={0} | all-to-all | bytes 786432 | tf_op jit(solution)/shard_map/all_to_all | solution.py:359
  135.8 1.4 shard_map.91
  (22 shorter events, 0.0 us)
Async XLA Ops:
  9.0 34.9 %all-to-all-start = ((bf16[12,16,1024]{2,1,0:T(8,128)(2,1)}), bf16[12,16,1024]{2,1,0:T(8,128)(2,1)S(1)}, u32[]{:S(2)}, u32[]{:S(2)}) async-start(bf16[12,16,1024]{2,1,0:T(8,128)(2,1)} %shard_map.86), calls=%async_computation | async-start | bytes 786432 | tf_op jit(solution)/shard_map/all_to_all | solution.py:257
  24.2 113.0 %reduce-scatter.2.cloned.1.call-start = ((), (), s32[]{:S(2)}) async-start(), calls=%async_computation.3 | async-start | bytes 3981312 | tf_op jit(solution)/shard_map/reduce_scatter | solution.py:345
  24.9 42.6 %copy-start = (bf16[384,3072]{1,0:T(8,128)(2,1)S(1)}, bf16[384,3072]{1,0:T(8,128)(2,1)}, u32[]{:S(2)}) copy-start(bf16[384,3072]{1,0:T(8,128)(2,1)} %refs_4_.1) | copy-start | bytes 7077892
  24.9 42.6 %copy-start.10 = (s32[2]{0:T(128)S(1)}, s32[2]{0:T(128)}, u32[]{:S(2)}) copy-start(s32[2]{0:T(128)} %pad_add_fusion.where_ref) | copy-start | bytes 28
  31.4 6.3 %collective-permute-start = (bf16[1536,256]{1,0:T(8,128)(2,1)}, bf16[1536,256]{1,0:T(8,128)(2,1)S(1)}, u32[]{:S(2)}, u32[]{:S(2)}) collective-permute-start(bf16[1536,256]{1,0:T(8,128)(2,1)} %get-tuple-element.21), channel_id=1, source_target_pairs={{0,48},{48,0},{1,49},{49,1},{2,50},{50,2},{3,51},{51,3},{4,52},{52... | collective-permute-start | bytes 2359304 | tf_op jit(solution)/shard_map/ppermute | solution.py:289
  33.3 3.7 %collective-permute-start.1 = (bf16[256,384]{1,0:T(8,128)(2,1)}, bf16[256,384]{1,0:T(8,128)(2,1)S(1)}, u32[]{:S(2)}, u32[]{:S(2)}) collective-permute-start(bf16[256,384]{1,0:T(8,128)(2,1)} %get-tuple-element.22.ho), channel_id=1, source_target_pairs={{0,48},{48,0},{1,49},{49,1},{2,50},{50,2},{3,51},{51,3},{4,52},{52... | collective-permute-start | bytes 589832 | tf_op jit(solution)/shard_map/ppermute | solution.py:289
  37.0 0.7 copy-start.7
  44.0 21.0 %collective-permute-start.2 = (bf16[192,1024]{1,0:T(8,128)(2,1)S(1)}, bf16[192,1024]{1,0:T(8,128)(2,1)S(1)}, u32[]{:S(2)}, u32[]{:S(2)}) collective-permute-start(bf16[192,1024]{1,0:T(8,128)(2,1)S(1)} %bitcast.8), channel_id=1, source_target_pairs={{0,3},{1,0},{2,1},{3,2},{4,7},{5,4},{6,5},{7,6},{8,11},{9,8},{10,9... | collective-permute-start | bytes 1179656 | tf_op jit(solution)/shard_map/ppermute | solution.py:292
  46.7 18.3 %collective-permute-start.3 = (bf16[192,1024]{1,0:T(8,128)(2,1)S(1)}, bf16[192,1024]{1,0:T(8,128)(2,1)S(1)}, u32[]{:S(2)}, u32[]{:S(2)}) collective-permute-start(bf16[192,1024]{1,0:T(8,128)(2,1)S(1)} %bitcast.9), channel_id=1, source_target_pairs={{0,2},{1,3},{2,0},{3,1},{4,6},{5,7},{6,4},{7,5},{8,10},{9,11},{10,... | collective-permute-start | bytes 1179656 | tf_op jit(solution)/shard_map/ppermute | solution.py:292
  49.7 17.8 %collective-permute-start.4 = (bf16[192,1024]{1,0:T(8,128)(2,1)S(1)}, bf16[192,1024]{1,0:T(8,128)(2,1)S(1)}, u32[]{:S(2)}, u32[]{:S(2)}) collective-permute-start(bf16[192,1024]{1,0:T(8,128)(2,1)S(1)} %bitcast.10), channel_id=1, source_target_pairs={{0,1},{1,2},{2,3},{3,0},{4,5},{5,6},{6,7},{7,4},{8,9},{9,10},{10,1... | collective-permute-start | bytes 1179656 | tf_op jit(solution)/shard_map/ppermute | solution.py:292
  67.5 1.0 copy-start.4
  68.5 1.0 copy-start.5
  69.5 6.0 %copy-start.1 = (bf16[384,3072]{1,0:T(8,128)(2,1)S(1)}, bf16[384,3072]{1,0:T(8,128)(2,1)}, u32[]{:S(2)}) copy-start(bf16[384,3072]{1,0:T(8,128)(2,1)} %wg_ref.1) | copy-start | bytes 7077892
  69.5 6.0 %copy-start.2 = (bf16[384,3072]{1,0:T(8,128)(2,1)S(1)}, bf16[384,3072]{1,0:T(8,128)(2,1)}, u32[]{:S(2)}) copy-start(bf16[384,3072]{1,0:T(8,128)(2,1)} %wu_ref.1) | copy-start | bytes 7077892
  73.4 5.3 %copy-start.3 = (bf16[1536,256]{1,0:T(8,128)(2,1)S(1)}, bf16[1536,256]{1,0:T(8,128)(2,1)}, u32[]{:S(2)}) copy-start(bf16[1536,256]{1,0:T(8,128)(2,1)} %get-tuple-element.35.xo) | copy-start | bytes 2359300
  73.5 5.3 %copy-start.6 = (bf16[256,384]{1,0:T(8,128)(2,1)S(1)}, bf16[256,384]{1,0:T(8,128)(2,1)}, u32[]{:S(2)}) copy-start(bf16[256,384]{1,0:T(8,128)(2,1)} %get-tuple-element.22.ho) | copy-start | bytes 589828
  73.5 5.3 %copy-start.8 = (bf16[256,384]{1,0:T(8,128)(2,1)S(1)}, bf16[256,384]{1,0:T(8,128)(2,1)}, u32[]{:S(2)}) copy-start(bf16[256,384]{1,0:T(8,128)(2,1)} %copy-done.7) | copy-start | bytes 589828
  73.5 5.2 %collective-permute-start.5 = (bf16[2304,256]{1,0:T(8,128)(2,1)S(1)}, bf16[2304,256]{1,0:T(8,128)(2,1)S(1)}, u32[]{:S(2)}, u32[]{:S(2)}) collective-permute-start(bf16[2304,256]{1,0:T(8,128)(2,1)S(1)} %get-tuple-element.26.both_ref.do), channel_id=1, source_target_pairs={{0,48},{48,0},{1,49},{49,1},{2,50},{50,2},{3,51},{51,3},{4,52},{52... | collective-permute-start | bytes 3538952 | tf_op jit(solution)/shard_map/ppermute | solution.py:289
  82.7 53.1 %copy-start.9 = (s32[10,2]{0,1:T(2,128)S(1)}, s32[10,2]{0,1:T(2,128)}, u32[]{:S(2)}) copy-start(s32[10,2]{0,1:T(2,128)} %param.8) | copy-start | bytes 244
  82.7 22.0 %collective-permute-start.6 = (bf16[64,3072]{1,0:T(8,128)(2,1)S(1)}, bf16[64,3072]{1,0:T(8,128)(2,1)S(1)}, u32[]{:S(2)}, u32[]{:S(2)}) collective-permute-start(bf16[64,3072]{1,0:T(8,128)(2,1)S(1)} %get-tuple-element.32), channel_id=1, source_target_pairs={{0,1},{1,2},{2,3},{3,0},{4,5},{5,6},{6,7},{7,4},{8,9},{9,10},{10,1... | collective-permute-start | bytes 1179656 | tf_op jit(solution)/shard_map/ppermute | solution.py:292
  87.3 17.5 %collective-permute-start.7 = (bf16[64,3072]{1,0:T(8,128)(2,1)S(1)}, bf16[64,3072]{1,0:T(8,128)(2,1)S(1)}, u32[]{:S(2)}, u32[]{:S(2)}) collective-permute-start(bf16[64,3072]{1,0:T(8,128)(2,1)S(1)} %get-tuple-element.33), channel_id=1, source_target_pairs={{0,2},{1,3},{2,0},{3,1},{4,6},{5,7},{6,4},{7,5},{8,10},{9,11},{10,... | collective-permute-start | bytes 1179656 | tf_op jit(solution)/shard_map/ppermute | solution.py:292
  89.4 20.9 %collective-permute-start.8 = (bf16[64,3072]{1,0:T(8,128)(2,1)S(1)}, bf16[64,3072]{1,0:T(8,128)(2,1)S(1)}, u32[]{:S(2)}, u32[]{:S(2)}) collective-permute-start(bf16[64,3072]{1,0:T(8,128)(2,1)S(1)} %get-tuple-element.34), channel_id=1, source_target_pairs={{0,3},{1,0},{2,1},{3,2},{4,7},{5,4},{6,5},{7,6},{8,11},{9,8},{10,9... | collective-permute-start | bytes 1179656 | tf_op jit(solution)/shard_map/ppermute | solution.py:292
Sparse Core Ops, SparseCore 0:
  82.8 50.8 reduce-scatter.1

commit v4 on v3

--- a/solution.py
+++ b/solution.py
@@ -118,6 +118,11 @@
         store.wait()
 
 
+def hold_body(act_at, slope_at, act_ref, slope_ref, sems):
+    for copy in start_all(((act_at, act_ref), (slope_at, slope_ref)), sems):
+        copy.wait()
+
+
 def picker(cap, block, used, packed, part):
     i = lax.broadcasted_iota(jnp.int32, (block, packed), 0)
     q = lax.broadcasted_iota(jnp.int32, (block, packed), 1)
@@ -125,8 +130,7 @@
 
 
 def middle_body(cap, block, used, own, where_ref, *refs):
-    *bufs, wd_at, act_at, slope_at, ship_ref, own_ref, dy, dyt, wd_ref, act_ref, slope_ref, arrived = refs
-    fetches = start_all(((wd_at, wd_ref), (act_at, act_ref), (slope_at, slope_ref)), arrived)
+    *bufs, wd_ref, act_ref, slope_ref, ship_ref, own_ref, dy, dyt = refs
     core = where_ref[1]
     packed, part = bufs[0].shape
     hid, width = wd_ref.shape
@@ -138,10 +142,7 @@
             dy[j * block : (j + 1) * block, p * part : (p + 1) * part] = jnp.dot(
                 pick, buf[...], preferred_element_type=F32
             ).astype(BF16)
-    fetches[0].wait()
     d_hidden = lax.dot_general(dy[...], wd_ref[...], NT, preferred_element_type=F32)
-    fetches[1].wait()
-    fetches[2].wait()
     both = jnp.concatenate([d_hidden * slope_ref[...], d_hidden * act_ref[...]], axis=1).astype(BF16)
     for k in range(2 * hid // rows):
         ship_ref[half + k * rows : half + (k + 1) * rows, :] = both[:, k * rows : (k + 1) * rows]
@@ -157,14 +158,16 @@
     return [ref[first + k * rows : first + (k + 1) * rows, :] for k in range(n // rows)]
 
 
-def back_body(block, both_ref, wg_ref, wu_ref, *outs):
-    hid = wg_ref.shape[0]
-    rows = both_ref.shape[1]
-    both = jnp.concatenate(columns(both_ref, 0, rows, 2 * hid), axis=1)
-    dx = jnp.dot(both[:, :hid], wg_ref[...], preferred_element_type=F32)
-    dx = (dx + jnp.dot(both[:, hid:], wu_ref[...], preferred_element_type=F32)).astype(BF16)
-    for j, out in enumerate(outs):
-        out[...] = dx[j * block : (j + 1) * block, :]
+def back_body(block, first, ship_ref, wg_ref, wu_ref, *outs):
+    hid, width = wg_ref.shape
+    step = 2 * TILE
+    both = jnp.concatenate(columns(ship_ref, first, ship_ref.shape[1], 2 * hid), axis=1)
+    for t in range(width // step):
+        cols = slice(t * step, (t + 1) * step)
+        dx = jnp.dot(both[:, :hid], wg_ref[:, cols], preferred_element_type=F32)
+        dx = (dx + jnp.dot(both[:, hid:], wu_ref[:, cols], preferred_element_type=F32)).astype(BF16)
+        for j, out in enumerate(outs):
+            out[:, cols] = dx[j * block : (j + 1) * block, :]
 
 
 def merge_body(cap, used, *refs):
@@ -190,21 +193,28 @@
         out_ref[k] = pack[k * SLOT_ROWS : (k + 1) * SLOT_ROWS, :]
 
 
-def terms_body(own, hid, xo, xp, yo, yp, do, dp, ho, hp, out):
-    rows = xo.shape[1]
-    d_own = jnp.concatenate(columns(do, 0, rows, 2 * hid), axis=1)
-    d_pair = jnp.concatenate(columns(dp, 0, rows, 2 * hid), axis=1)
-    both = jnp.dot(xo[...], d_own, preferred_element_type=F32)
-    both = both + jnp.dot(xp[...], d_pair, preferred_element_type=F32)
-    down = jnp.dot(yo[...], ho[...], preferred_element_type=F32)
-    down = down + jnp.dot(yp[...], hp[...], preferred_element_type=F32)
-    both = both.astype(BF16)
-    down = down.astype(BF16)
-    for g in range(out.shape[0]):
-        rows = slice(g * own, (g + 1) * own)
-        out[g, 0] = both[rows, :hid]
-        out[g, 1] = both[rows, hid:]
-        out[g, 2] = down[rows, :]
+def terms_body(own, hid, steps, xo, xp, yo, ship, got, ho, hp, out_at, stage, sems):
+    half, rows = xo.shape
+    per = out_at.shape[0] // steps
+    depth = per * own
+    d_own = jnp.concatenate(columns(ship, half, rows, 2 * hid), axis=1)
+    d_pair = jnp.concatenate(columns(got, half, rows, 2 * hid), axis=1)
+    stores = []
+    for s in range(steps):
+        here = slice(s * depth, (s + 1) * depth)
+        both = jnp.dot(xo[here, :], d_own, preferred_element_type=F32)
+        both = (both + jnp.dot(xp[here, :], d_pair, preferred_element_type=F32)).astype(BF16)
+        down = jnp.dot(yo[here, :], ho[...], preferred_element_type=F32)
+        down = (down + jnp.dot(got[here, :], hp[...], preferred_element_type=F32)).astype(BF16)
+        for g in range(per):
+            part = slice(g * own, (g + 1) * own)
+            stage[s * per + g, 0] = both[part, :hid]
+            stage[s * per + g, 1] = both[part, hid:]
+            stage[s * per + g, 2] = down[part, :]
+        groups = pl.ds(s * per, per)
+        stores += start_all(((stage.at[groups], out_at.at[groups]),), sems, s)
+    for store in stores:
+        store.wait()
 
 
 def final_body(cap, routes_ref, back_ref, out_ref, sums, grads):
@@ -297,51 +307,44 @@
     first, x_pair, hidden_pair = lax.optimization_barrier((first, x_pair, hidden_pair))
     mine = first.reshape(packed, part)
     bufs = [mine] + [shift(mine, -j) for j in range(1, n_x)]
+    bufs[1], act, slope = lax.optimization_barrier((bufs[1], act, slope))
+    act, slope = call(
+        hold_body,
+        (shape((rows, hid), F32), shape((rows, hid), F32)),
+        [HBM] * 2,
+        [pltpu.SemaphoreType.DMA((2,))],
+        moved=16 * rows * hid,
+    )(act, slope)
     ship, y_own = call(
         functools.partial(middle_body, cap, block, used, own),
         (shape((half + 2 * hid, rows), BF16), shape((half, rows), BF16)),
-        [SMEM] + [VMEM] * n_x + [HBM] * 3,
-        [
-            pltpu.VMEM((rows, width), BF16),
-            pltpu.VMEM((width, rows), BF16),
-            pltpu.VMEM(w_down.shape, BF16),
-            pltpu.VMEM((rows, hid), F32),
-            pltpu.VMEM((rows, hid), F32),
-            pltpu.SemaphoreType.DMA((3,)),
-        ],
-        mib=16,
+        [SMEM] + [VMEM] * (n_x + 3),
+        [pltpu.VMEM((rows, width), BF16), pltpu.VMEM((width, rows), BF16)],
         flops=2 * rows * width * (hid + rows),
         moved=2 * width * (hid + 2 * rows) + 10 * rows * hid,
     )(where, *bufs, w_down, act, slope)
     got = swap(ship)
 
-    step = 512
-    late = half // (2 * hid)
     back = call(
-        functools.partial(back_body, block),
+        functools.partial(back_body, block, half),
         tuple(shape((block, width), BF16) for _ in range(n_x)),
-        [pl.BlockSpec((2 * hid, rows), lambda g: (late, 0))] + [pl.BlockSpec((hid, step), lambda g: (0, g))] * 2,
+        [VMEM] * 3,
         flops=2 * rows * width * 2 * hid,
         moved=2 * width * (2 * hid + rows),
-        out_specs=tuple(pl.BlockSpec((block, step), lambda g: (0, g)) for _ in range(n_x)),
-        grid=(width // step,),
     )(ship, w_gate, w_up)
     got, back = lax.optimization_barrier((got, back))
 
     steps = n_y // 2
-    per = n_y // steps
-    feature = pl.BlockSpec((per * own, rows), lambda g: (g, 0))
-    tail = pl.BlockSpec((2 * hid, rows), lambda g: (late, 0))
-    whole = pl.BlockSpec((rows, hid), lambda g: (0, 0))
     terms = call(
-        functools.partial(terms_body, own, hid),
+        functools.partial(terms_body, own, hid, steps),
         shape((n_y, 3, own, hid), BF16),
-        [feature] * 4 + [tail] * 2 + [whole] * 2,
+        [VMEM] * 7,
+        [pltpu.VMEM((n_y, 3, own, hid), BF16), pltpu.SemaphoreType.DMA((steps,))],
         flops=2 * 2 * rows * half * 3 * hid,
         moved=2 * half * (3 * hid + 4 * rows),
-        out_specs=pl.BlockSpec((per, 3, own, hid), lambda g: (g, 0, 0, 0)),
-        grid=(steps,),
-    )(x_own, x_pair, y_own, got, ship, got, hidden, hidden_pair)
+        mib=24,
+        out_specs=HBM,
+    )(x_own, x_pair, y_own, ship, got, hidden, hidden_pair)
     shares = lax.psum_scatter(
         terms.reshape(n_y * 3 * own, hid), "y", scatter_dimension=0, tiled=True
     )

time: 145 us -> 140 us (0.966)
  Pallas kernels: 21.2 us -> 18.5 us
  waiting for transfers between devices: 39.7 us -> 38 us
    ppermute x6, waiting for transfers between devices: 32.1 us -> 29.4 us  [shift(): return lax.ppermute(v, 'x', [(i, (i + by) % n_x) for i in range(n_x)])]
    pallas_call x2 -> x3, Pallas kernels: 7.07 us -> 5.34 us  [the longest x1 3.17 us: per_device(): call(functools.partial(terms_body, own, hid, steps), shape((n_y, 3, own,...]
  transfers between devices with their start and end apart: 11 -> 11, of which waited for: 6 -> 7; matrix products, arithmetic and copies ran while one was open for 0% -> 0% of each run, Pallas kernels for 8% -> 8%
where the time goes in v4:
time: 140 us; the launch traced here: 139 us
  starting transfers between devices  40.6 us (29%)
  waiting for transfers between devices  38 us (27%)
  blocking collectives  24.9 us (18%)
  Pallas kernels  18.5 us (13%)
  between operations  14.2 us (10%)
  local copies, waits for them, and re-layouts  2.71 us (2%)
    ppermute x6, waiting for transfers between devices, shift(): return lax.ppermute(v, 'x', [(i, (i + by) % n_x) for i in range(n_x)])  29.4 us
    all_to_all x1, blocking collectives, per_device(): lax.all_to_all(added, 'z', split_axis=0, concat_axis=0, tiled=True)  24.9 us
    ppermute x6, starting transfers between devices, shift(): return lax.ppermute(v, 'x', [(i, (i + by) % n_x) for i in range(n_x)])  19 us
    all_to_all x1, starting transfers between devices, per_device(): first = lax.all_to_all(sent, 'z', split_axis=0, concat_axis=0, tiled=True)  15.2 us
    pallas_call x1, Pallas kernels, per_device(): call(functools.partial(early_body, cap, n_x, block, own), (shape((half, r...  6.46 us
    ppermute x3, starting transfers between devices, swap(): return lax.ppermute(v, 'c', [(i, (i + 1) % n_c) for i in range(n_c)])  6.38 us
    all_to_all x1, waiting for transfers between devices, per_device(): first = lax.all_to_all(sent, 'z', split_axis=0, concat_axis=0, tiled=True)  6.35 us
    pallas_call x1, Pallas kernels, per_device(): call(functools.partial(terms_body, own, hid, steps), shape((n_y, 3, own,...  3.17 us
  transfers between devices with their start and end apart: 11, of which 7 were waited for; matrix products, arithmetic and copies ran while one was open for 0% of the time, Pallas kernels for 8%

profile of v4, /device:TPU:6, one launch (start us, length us, event | category | flops | bytes accessed | tf_op | source)
XLA Modules:
  0.0 139.5 jit_solution(5326991171111571124)
XLA Ops:
  7.2 1.9 %shard_map.86 = bf16[12,16,1024]{2,1,0:T(8,128)(2,1)} custom-call(s32[2,10]{1,0:T(2,128)} %bitcast.12, f32[2,10]{1,0:T(2,128)} %bitcast.14, bf16[10,3072]{1,0:T(8,128)(2,1)} %d_ref.1), custom_call_target="tpu_custom_call" | custom-call | bytes 500000 | tf_op jit(solution)/shard_map/pallas_call | solution.py:259
  9.0 15.2 %all-to-all-start = ((bf16[12,16,1024]{2,1,0:T(8,128)(2,1)}), bf16[12,16,1024]{2,1,0:T(8,128)(2,1)S(1)}, u32[]{:S(2)}, u32[]{:S(2)}) async-start(bf16[12,16,1024]{2,1,0:T(8,128)(2,1)} %shard_map.86), calls=%async_computation | async-start | bytes 786432 | tf_op jit(solution)/shard_map/all_to_all | solution.py:267
  24.2 0.0 reduce-scatter.2.cloned.1.call-start
  24.3 0.6 pad_add_fusion.where_ref
  24.8 6.5 %shard_map.87 = (bf16[1536,256]{1,0:T(8,128)(2,1)}, bf16[1536,256]{1,0:T(8,128)(2,1)}, f32[256,384]{1,0:T(8,128)}, f32[256,384]{1,0:T(8,128)}, bf16[256,384]{1,0:T(8,128)(2,1)}) custom-call(s32[2]{0:T(128)} %pad_add_fusion.where_ref, bf16[240,3072]{1,0:T(8,128)(2,1)} %bitcast.15, bf16[384,3072]{1,0:T(8,128)(2,1)} %wg_ref.1, bf16[384,3072]{1,0:T(8,128)(2,1)} %wu_ref.1), custom_call_target="tpu_custom_call" | custom-call | flops 2013265920 | bytes 8847360 | tf_op jit(solution)/shard_map/pallas_call | solution.py:269
  31.3 1.9 %collective-permute-start = (bf16[1536,256]{1,0:T(8,128)(2,1)}, bf16[1536,256]{1,0:T(8,128)(2,1)S(1)}, u32[]{:S(2)}, u32[]{:S(2)}) collective-permute-start(bf16[1536,256]{1,0:T(8,128)(2,1)} %get-tuple-element.26), channel_id=1, source_target_pairs={{0,48},{48,0},{1,49},{49,1},{2,50},{50,2},{3,51},{51,3},{4,52},{52... | collective-permute-start | bytes 2359304 | tf_op jit(solution)/shard_map/ppermute | solution.py:299
  33.2 2.4 %collective-permute-start.1 = (bf16[256,384]{1,0:T(8,128)(2,1)}, bf16[256,384]{1,0:T(8,128)(2,1)S(1)}, u32[]{:S(2)}, u32[]{:S(2)}) collective-permute-start(bf16[256,384]{1,0:T(8,128)(2,1)} %get-tuple-element.27.ho), channel_id=1, source_target_pairs={{0,48},{48,0},{1,49},{49,1},{2,50},{50,2},{3,51},{51,3},{4,52},{52... | collective-permute-start | bytes 589832 | tf_op jit(solution)/shard_map/ppermute | solution.py:299
  35.7 1.3 collective-permute-done.1.hp
  36.9 0.7 copy-done.7
  37.6 6.4 %all-to-all-done = bf16[12,16,1024]{2,1,0:T(8,128)(2,1)S(1)} async-done(((bf16[12,16,1024]{2,1,0:T(8,128)(2,1)}), bf16[12,16,1024]{2,1,0:T(8,128)(2,1)S(1)}, u32[]{:S(2)}, u32[]{:S(2)}) %all-to-all-start) | async-done | bytes 393248 | tf_op jit(solution)/shard_map/all_to_all | solution.py:267
  44.0 2.7 %collective-permute-start.2 = (bf16[192,1024]{1,0:T(8,128)(2,1)S(1)}, bf16[192,1024]{1,0:T(8,128)(2,1)S(1)}, u32[]{:S(2)}, u32[]{:S(2)}) collective-permute-start(bf16[192,1024]{1,0:T(8,128)(2,1)S(1)} %bitcast.8), channel_id=1, source_target_pairs={{0,3},{1,0},{2,1},{3,2},{4,7},{5,4},{6,5},{7,6},{8,11},{9,8},{10,9... | collective-permute-start | bytes 1179656 | tf_op jit(solution)/shard_map/ppermute | solution.py:302
  46.7 3.0 %collective-permute-start.3 = (bf16[192,1024]{1,0:T(8,128)(2,1)S(1)}, bf16[192,1024]{1,0:T(8,128)(2,1)S(1)}, u32[]{:S(2)}, u32[]{:S(2)}) collective-permute-start(bf16[192,1024]{1,0:T(8,128)(2,1)S(1)} %bitcast.9), channel_id=1, source_target_pairs={{0,2},{1,3},{2,0},{3,1},{4,6},{5,7},{6,4},{7,5},{8,10},{9,11},{10,... | collective-permute-start | bytes 1179656 | tf_op jit(solution)/shard_map/ppermute | solution.py:302
  49.7 4.0 %collective-permute-start.4 = (bf16[192,1024]{1,0:T(8,128)(2,1)S(1)}, bf16[192,1024]{1,0:T(8,128)(2,1)S(1)}, u32[]{:S(2)}, u32[]{:S(2)}) collective-permute-start(bf16[192,1024]{1,0:T(8,128)(2,1)S(1)} %bitcast.10), channel_id=1, source_target_pairs={{0,1},{1,2},{2,3},{3,0},{4,5},{5,6},{6,7},{7,4},{8,9},{9,10},{10,1... | collective-permute-start | bytes 1179656 | tf_op jit(solution)/shard_map/ppermute | solution.py:302
  53.7 11.2 %collective-permute-done.2.refs_1_ = bf16[192,1024]{1,0:T(8,128)(2,1)S(1)} collective-permute-done((bf16[192,1024]{1,0:T(8,128)(2,1)S(1)}, bf16[192,1024]{1,0:T(8,128)(2,1)S(1)}, u32[]{:S(2)}, u32[]{:S(2)}) %collective-permute-start.2) | collective-permute-done | bytes 393248 | tf_op jit(solution)/shard_map/ppermute | solution.py:302
  65.0 1.0 copy-done.4
  66.0 1.0 copy-done.5
  67.0 0.4 shard_map.88
  67.4 0.1 collective-permute-done.4.refs_3_
  67.5 2.9 %shard_map.89 = (bf16[2304,256]{1,0:T(8,128)(2,1)S(1)}, bf16[1536,256]{1,0:T(8,128)(2,1)S(1)}) custom-call(s32[2]{0:T(128)S(1)} %copy-done.10, bf16[192,1024]{1,0:T(8,128)(2,1)S(1)} %bitcast.11, bf16[192,1024]{1,0:T(8,128)(2,1)S(1)} %collective-permute-done.2.refs_1_, bf16[192,1024]{1,0:T(8,128)(2,1)S(1)} %collective-permute-done.3.refs_2_, ...), custom_call_target="tpu_custom_call" | custom-call | flops 1006632960 | bytes 6488064 | tf_op jit(solution)/shard_map/pallas_call | solution.py:318
  70.5 2.1 %collective-permute-start.5 = (bf16[2304,256]{1,0:T(8,128)(2,1)S(1)}, bf16[2304,256]{1,0:T(8,128)(2,1)S(1)}, u32[]{:S(2)}, u32[]{:S(2)}) collective-permute-start(bf16[2304,256]{1,0:T(8,128)(2,1)S(1)} %get-tuple-element.36.ship_ref.ship), channel_id=1, source_target_pairs={{0,48},{48,0},{1,49},{49,1},{2,50},{50,2},{3,51},{51,3},{4,52},{52... | collective-permute-start | bytes 3538952 | tf_op jit(solution)/shard_map/ppermute | solution.py:299
  72.6 1.8 %shard_map.90 = (bf16[64,3072]{1,0:T(8,128)(2,1)S(1)}, bf16[64,3072]{1,0:T(8,128)(2,1)S(1)}, bf16[64,3072]{1,0:T(8,128)(2,1)S(1)}, bf16[64,3072]{1,0:T(8,128)(2,1)S(1)}) custom-call(bf16[2304,256]{1,0:T(8,128)(2,1)S(1)} %get-tuple-element.36.ship_ref.ship, bf16[384,3072]{1,0:T(8,128)(2,1)S(1)} %copy-done.1, bf16[384,3072]{1,0:T(8,128)(2,1)S(1)} %copy-done.2), custom_call_target="tpu_custom_call" | custom-call | flops 1207959552 | bytes 6291456 | tf_op jit(solution)/shard_map/pallas_call | solution.py:328
  74.4 1.0 collective-permute-done.5.got
  75.4 3.2 %shard_map.93 = bf16[8,3,192,384]{3,2,1,0:T(8,128)(2,1)} custom-call(bf16[1536,256]{1,0:T(8,128)(2,1)S(1)} %copy-done.3, bf16[1536,256]{1,0:T(8,128)(2,1)S(1)} %collective-permute-done.xp, bf16[1536,256]{1,0:T(8,128)(2,1)S(1)} %get-tuple-element.47.yo, bf16[2304,256]{1,0:T(8,128)(2,1)S(1)} %get-tuple-element.36.ship_ref.ship, ...), custom_call_target="tpu_custom_call" | custom-call | flops 1811939328 | bytes 6684672 | tf_op jit(solution)/shard_map/pallas_call | solution.py:338
  78.6 0.0 reduce-scatter.2.cloned.1.call-update
  78.6 4.5 %collective-permute-start.6 = (bf16[64,3072]{1,0:T(8,128)(2,1)S(1)}, bf16[64,3072]{1,0:T(8,128)(2,1)S(1)}, u32[]{:S(2)}, u32[]{:S(2)}) collective-permute-start(bf16[64,3072]{1,0:T(8,128)(2,1)S(1)} %get-tuple-element.42), channel_id=1, source_target_pairs={{0,1},{1,2},{2,3},{3,0},{4,5},{5,6},{6,7},{7,4},{8,9},{9,10},{10,1... | collective-permute-start | bytes 1179656 | tf_op jit(solution)/shard_map/ppermute | solution.py:302
  83.1 2.1 %collective-permute-start.7 = (bf16[64,3072]{1,0:T(8,128)(2,1)S(1)}, bf16[64,3072]{1,0:T(8,128)(2,1)S(1)}, u32[]{:S(2)}, u32[]{:S(2)}) collective-permute-start(bf16[64,3072]{1,0:T(8,128)(2,1)S(1)} %get-tuple-element.43), channel_id=1, source_target_pairs={{0,2},{1,3},{2,0},{3,1},{4,6},{5,7},{6,4},{7,5},{8,10},{9,11},{10,... | collective-permute-start | bytes 1179656 | tf_op jit(solution)/shard_map/ppermute | solution.py:302
  85.3 2.6 %collective-permute-start.8 = (bf16[64,3072]{1,0:T(8,128)(2,1)S(1)}, bf16[64,3072]{1,0:T(8,128)(2,1)S(1)}, u32[]{:S(2)}, u32[]{:S(2)}) collective-permute-start(bf16[64,3072]{1,0:T(8,128)(2,1)S(1)} %get-tuple-element.44), channel_id=1, source_target_pairs={{0,3},{1,0},{2,1},{3,2},{4,7},{5,4},{6,5},{7,6},{8,11},{9,8},{10,9... | collective-permute-start | bytes 1179656 | tf_op jit(solution)/shard_map/ppermute | solution.py:302
  87.8 12.4 %collective-permute-done.6.refs_1_ = bf16[64,3072]{1,0:T(8,128)(2,1)S(1)} collective-permute-done((bf16[64,3072]{1,0:T(8,128)(2,1)S(1)}, bf16[64,3072]{1,0:T(8,128)(2,1)S(1)}, u32[]{:S(2)}, u32[]{:S(2)}) %collective-permute-start.6) | collective-permute-done | bytes 393248 | tf_op jit(solution)/shard_map/ppermute | solution.py:302
  100.3 5.6 %collective-permute-done.8.refs_3_ = bf16[64,3072]{1,0:T(8,128)(2,1)S(1)} collective-permute-done((bf16[64,3072]{1,0:T(8,128)(2,1)S(1)}, bf16[64,3072]{1,0:T(8,128)(2,1)S(1)}, u32[]{:S(2)}, u32[]{:S(2)}) %collective-permute-start.8) | collective-permute-done | bytes 393248 | tf_op jit(solution)/shard_map/ppermute | solution.py:302
  105.8 0.5 shard_map.91
  106.4 24.9 %all_to_all.10.back_ref = bf16[12,16,1024]{2,1,0:T(8,128)(2,1)S(1)} all-to-all(bf16[12,16,1024]{2,1,0:T(8,128)(2,1)S(1)} %shard_map.91), channel_id=1, replica_groups=mesh['y'=8,'c'=2,'z'=12,'x'=4] {'z'}, dimensions={0} | all-to-all | bytes 786432 | tf_op jit(solution)/shard_map/all_to_all | solution.py:362
  131.2 1.4 shard_map.92
  (23 shorter events, 0.0 us)
Async XLA Ops:
  9.0 34.9 %all-to-all-start = ((bf16[12,16,1024]{2,1,0:T(8,128)(2,1)}), bf16[12,16,1024]{2,1,0:T(8,128)(2,1)S(1)}, u32[]{:S(2)}, u32[]{:S(2)}) async-start(bf16[12,16,1024]{2,1,0:T(8,128)(2,1)} %shard_map.86), calls=%async_computation | async-start | bytes 786432 | tf_op jit(solution)/shard_map/all_to_all | solution.py:267
  24.2 108.4 %reduce-scatter.2.cloned.1.call-start = ((), (), s32[]{:S(2)}) async-start(), calls=%async_computation.3 | async-start | bytes 3981312 | tf_op jit(solution)/shard_map/reduce_scatter | solution.py:348
  24.8 42.7 %copy-start = (bf16[384,3072]{1,0:T(8,128)(2,1)S(1)}, bf16[384,3072]{1,0:T(8,128)(2,1)}, u32[]{:S(2)}) copy-start(bf16[384,3072]{1,0:T(8,128)(2,1)} %refs_4_.1) | copy-start | bytes 7077892
  24.8 42.7 %copy-start.10 = (s32[2]{0:T(128)S(1)}, s32[2]{0:T(128)}, u32[]{:S(2)}) copy-start(s32[2]{0:T(128)} %pad_add_fusion.where_ref) | copy-start | bytes 28
  31.3 6.3 %collective-permute-start = (bf16[1536,256]{1,0:T(8,128)(2,1)}, bf16[1536,256]{1,0:T(8,128)(2,1)S(1)}, u32[]{:S(2)}, u32[]{:S(2)}) collective-permute-start(bf16[1536,256]{1,0:T(8,128)(2,1)} %get-tuple-element.26), channel_id=1, source_target_pairs={{0,48},{48,0},{1,49},{49,1},{2,50},{50,2},{3,51},{51,3},{4,52},{52... | collective-permute-start | bytes 2359304 | tf_op jit(solution)/shard_map/ppermute | solution.py:299
  33.2 3.7 %collective-permute-start.1 = (bf16[256,384]{1,0:T(8,128)(2,1)}, bf16[256,384]{1,0:T(8,128)(2,1)S(1)}, u32[]{:S(2)}, u32[]{:S(2)}) collective-permute-start(bf16[256,384]{1,0:T(8,128)(2,1)} %get-tuple-element.27.ho), channel_id=1, source_target_pairs={{0,48},{48,0},{1,49},{49,1},{2,50},{50,2},{3,51},{51,3},{4,52},{52... | collective-permute-start | bytes 589832 | tf_op jit(solution)/shard_map/ppermute | solution.py:299
  36.9 0.7 copy-start.7
  44.0 21.0 %collective-permute-start.2 = (bf16[192,1024]{1,0:T(8,128)(2,1)S(1)}, bf16[192,1024]{1,0:T(8,128)(2,1)S(1)}, u32[]{:S(2)}, u32[]{:S(2)}) collective-permute-start(bf16[192,1024]{1,0:T(8,128)(2,1)S(1)} %bitcast.8), channel_id=1, source_target_pairs={{0,3},{1,0},{2,1},{3,2},{4,7},{5,4},{6,5},{7,6},{8,11},{9,8},{10,9... | collective-permute-start | bytes 1179656 | tf_op jit(solution)/shard_map/ppermute | solution.py:302
  46.7 20.7 %collective-permute-start.3 = (bf16[192,1024]{1,0:T(8,128)(2,1)S(1)}, bf16[192,1024]{1,0:T(8,128)(2,1)S(1)}, u32[]{:S(2)}, u32[]{:S(2)}) collective-permute-start(bf16[192,1024]{1,0:T(8,128)(2,1)S(1)} %bitcast.9), channel_id=1, source_target_pairs={{0,2},{1,3},{2,0},{3,1},{4,6},{5,7},{6,4},{7,5},{8,10},{9,11},{10,... | collective-permute-start | bytes 1179656 | tf_op jit(solution)/shard_map/ppermute | solution.py:302
  49.7 17.8 %collective-permute-start.4 = (bf16[192,1024]{1,0:T(8,128)(2,1)S(1)}, bf16[192,1024]{1,0:T(8,128)(2,1)S(1)}, u32[]{:S(2)}, u32[]{:S(2)}) collective-permute-start(bf16[192,1024]{1,0:T(8,128)(2,1)S(1)} %bitcast.10), channel_id=1, source_target_pairs={{0,1},{1,2},{2,3},{3,0},{4,5},{5,6},{6,7},{7,4},{8,9},{9,10},{10,1... | collective-permute-start | bytes 1179656 | tf_op jit(solution)/shard_map/ppermute | solution.py:302
  65.0 1.0 copy-start.4
  66.0 1.0 copy-start.5
  67.5 5.0 %copy-start.1 = (bf16[384,3072]{1,0:T(8,128)(2,1)S(1)}, bf16[384,3072]{1,0:T(8,128)(2,1)}, u32[]{:S(2)}) copy-start(bf16[384,3072]{1,0:T(8,128)(2,1)} %wg_ref.1) | copy-start | bytes 7077892
  67.5 5.0 %copy-start.2 = (bf16[384,3072]{1,0:T(8,128)(2,1)S(1)}, bf16[384,3072]{1,0:T(8,128)(2,1)}, u32[]{:S(2)}) copy-start(bf16[384,3072]{1,0:T(8,128)(2,1)} %wu_ref.1) | copy-start | bytes 7077892
  70.5 4.9 %copy-start.3 = (bf16[1536,256]{1,0:T(8,128)(2,1)S(1)}, bf16[1536,256]{1,0:T(8,128)(2,1)}, u32[]{:S(2)}) copy-start(bf16[1536,256]{1,0:T(8,128)(2,1)} %get-tuple-element.45.xo) | copy-start | bytes 2359300
  70.5 4.9 %copy-start.6 = (bf16[256,384]{1,0:T(8,128)(2,1)S(1)}, bf16[256,384]{1,0:T(8,128)(2,1)}, u32[]{:S(2)}) copy-start(bf16[256,384]{1,0:T(8,128)(2,1)} %get-tuple-element.27.ho) | copy-start | bytes 589828
  70.5 4.9 %copy-start.8 = (bf16[256,384]{1,0:T(8,128)(2,1)S(1)}, bf16[256,384]{1,0:T(8,128)(2,1)}, u32[]{:S(2)}) copy-start(bf16[256,384]{1,0:T(8,128)(2,1)} %copy-done.7) | copy-start | bytes 589828
  70.5 4.9 %collective-permute-start.5 = (bf16[2304,256]{1,0:T(8,128)(2,1)S(1)}, bf16[2304,256]{1,0:T(8,128)(2,1)S(1)}, u32[]{:S(2)}, u32[]{:S(2)}) collective-permute-start(bf16[2304,256]{1,0:T(8,128)(2,1)S(1)} %get-tuple-element.36.ship_ref.ship), channel_id=1, source_target_pairs={{0,48},{48,0},{1,49},{49,1},{2,50},{50,2},{3,51},{51,3},{4,52},{52... | collective-permute-start | bytes 3538952 | tf_op jit(solution)/shard_map/ppermute | solution.py:299
  78.6 52.7 %copy-start.9 = (s32[10,2]{0,1:T(2,128)S(1)}, s32[10,2]{0,1:T(2,128)}, u32[]{:S(2)}) copy-start(s32[10,2]{0,1:T(2,128)} %param.8) | copy-start | bytes 244
  78.6 21.7 %collective-permute-start.6 = (bf16[64,3072]{1,0:T(8,128)(2,1)S(1)}, bf16[64,3072]{1,0:T(8,128)(2,1)S(1)}, u32[]{:S(2)}, u32[]{:S(2)}) collective-permute-start(bf16[64,3072]{1,0:T(8,128)(2,1)S(1)} %get-tuple-element.42), channel_id=1, source_target_pairs={{0,1},{1,2},{2,3},{3,0},{4,5},{5,6},{6,7},{7,4},{8,9},{9,10},{10,1... | collective-permute-start | bytes 1179656 | tf_op jit(solution)/shard_map/ppermute | solution.py:302
  83.1 17.1 %collective-permute-start.7 = (bf16[64,3072]{1,0:T(8,128)(2,1)S(1)}, bf16[64,3072]{1,0:T(8,128)(2,1)S(1)}, u32[]{:S(2)}, u32[]{:S(2)}) collective-permute-start(bf16[64,3072]{1,0:T(8,128)(2,1)S(1)} %get-tuple-element.43), channel_id=1, source_target_pairs={{0,2},{1,3},{2,0},{3,1},{4,6},{5,7},{6,4},{7,5},{8,10},{9,11},{10,... | collective-permute-start | bytes 1179656 | tf_op jit(solution)/shard_map/ppermute | solution.py:302
  85.3 20.6 %collective-permute-start.8 = (bf16[64,3072]{1,0:T(8,128)(2,1)S(1)}, bf16[64,3072]{1,0:T(8,128)(2,1)S(1)}, u32[]{:S(2)}, u32[]{:S(2)}) collective-permute-start(bf16[64,3072]{1,0:T(8,128)(2,1)S(1)} %get-tuple-element.44), channel_id=1, source_target_pairs={{0,3},{1,0},{2,1},{3,2},{4,7},{5,4},{6,5},{7,6},{8,11},{9,8},{10,9... | collective-permute-start | bytes 1179656 | tf_op jit(solution)/shard_map/ppermute | solution.py:302
Sparse Core Ops, SparseCore 0:
  78.7 50.6 reduce-scatter.1

commit v5 on v4

--- a/solution.py
+++ b/solution.py
@@ -301,12 +301,15 @@
     def shift(v, by):
         return lax.ppermute(v, "x", [(i, (i + by) % n_x) for i in range(n_x)])
 
+    nearest = sorted(range(1, n_x), key=lambda j: min(j, n_x - j))
+
     x_pair = swap(x_other)
     hidden_pair = swap(hidden)
 
     first, x_pair, hidden_pair = lax.optimization_barrier((first, x_pair, hidden_pair))
     mine = first.reshape(packed, part)
-    bufs = [mine] + [shift(mine, -j) for j in range(1, n_x)]
+    moved = {j: shift(mine, -j) for j in nearest}
+    bufs = [mine] + [moved[j] for j in range(1, n_x)]
     bufs[1], act, slope = lax.optimization_barrier((bufs[1], act, slope))
     act, slope = call(
         hold_body,
@@ -350,7 +353,7 @@
     )
     weight_grads = shares.reshape(3, own, hid)
 
-    arrived = [back[0]] + [shift(back[j], j) for j in range(1, n_x)]
+    arrived = [back[0]] + [shift(back[j], j) for j in nearest]
     added = call(
         functools.partial(merge_body, cap, used),
         shape((n_z, SLOT_ROWS, part), BF16),

time: 140 us -> 139 us (level)
  no operation moved by 1% of the time
where the time goes in v5:
time: 139 us; the launch traced here: 138 us
  starting transfers between devices  41.2 us (30%)
  waiting for transfers between devices  37.1 us (27%)
  blocking collectives  24.1 us (17%)
  Pallas kernels  18.5 us (13%)
  between operations  14.2 us (10%)
  local copies, waits for them, and re-layouts  2.71 us (2%)
    ppermute x6, waiting for transfers between devices, shift(): return lax.ppermute(v, 'x', [(i, (i + by) % n_x) for i in range(n_x)])  28.5 us
    all_to_all x1, blocking collectives, per_device(): lax.all_to_all(added, 'z', split_axis=0, concat_axis=0, tiled=True)  24.1 us
    ppermute x6, starting transfers between devices, shift(): return lax.ppermute(v, 'x', [(i, (i + by) % n_x) for i in range(n_x)])  19.6 us
    all_to_all x1, starting transfers between devices, per_device(): first = lax.all_to_all(sent, 'z', split_axis=0, concat_axis=0, tiled=True)  15.2 us
    pallas_call x1, Pallas kernels, per_device(): call(functools.partial(early_body, cap, n_x, block, own), (shape((half, r...  6.46 us
    ppermute x3, starting transfers between devices, swap(): return lax.ppermute(v, 'c', [(i, (i + 1) % n_c) for i in range(n_c)])  6.38 us
    all_to_all x1, waiting for transfers between devices, per_device(): first = lax.all_to_all(sent, 'z', split_axis=0, concat_axis=0, tiled=True)  6.35 us
    pallas_call x1, Pallas kernels, per_device(): call(functools.partial(terms_body, own, hid, steps), shape((n_y, 3, own,...  3.17 us
  transfers between devices with their start and end apart: 11, of which 7 were waited for; matrix products, arithmetic and copies ran while one was open for 0% of the time, Pallas kernels for 8%

profile of v5, /device:TPU:6, one launch (start us, length us, event | category | flops | bytes accessed | tf_op | source)
XLA Modules:
  0.0 138.4 jit_solution(5184654601673010948)
XLA Ops:
  7.2 1.9 %shard_map.86 = bf16[12,16,1024]{2,1,0:T(8,128)(2,1)} custom-call(s32[2,10]{1,0:T(2,128)} %bitcast.12, f32[2,10]{1,0:T(2,128)} %bitcast.14, bf16[10,3072]{1,0:T(8,128)(2,1)} %d_ref.1), custom_call_target="tpu_custom_call" | custom-call | bytes 500000 | tf_op jit(solution)/shard_map/pallas_call | solution.py:259
  9.0 15.2 %all-to-all-start = ((bf16[12,16,1024]{2,1,0:T(8,128)(2,1)}), bf16[12,16,1024]{2,1,0:T(8,128)(2,1)S(1)}, u32[]{:S(2)}, u32[]{:S(2)}) async-start(bf16[12,16,1024]{2,1,0:T(8,128)(2,1)} %shard_map.86), calls=%async_computation | async-start | bytes 786432 | tf_op jit(solution)/shard_map/all_to_all | solution.py:267
  24.2 0.0 reduce-scatter.2.cloned.1.call-start
  24.3 0.6 pad_add_fusion.where_ref
  24.8 6.5 %shard_map.87 = (bf16[1536,256]{1,0:T(8,128)(2,1)}, bf16[1536,256]{1,0:T(8,128)(2,1)}, f32[256,384]{1,0:T(8,128)}, f32[256,384]{1,0:T(8,128)}, bf16[256,384]{1,0:T(8,128)(2,1)}) custom-call(s32[2]{0:T(128)} %pad_add_fusion.where_ref, bf16[240,3072]{1,0:T(8,128)(2,1)} %bitcast.15, bf16[384,3072]{1,0:T(8,128)(2,1)} %wg_ref.1, bf16[384,3072]{1,0:T(8,128)(2,1)} %wu_ref.1), custom_call_target="tpu_custom_call" | custom-call | flops 2013265920 | bytes 8847360 | tf_op jit(solution)/shard_map/pallas_call | solution.py:269
  31.3 1.9 %collective-permute-start = (bf16[1536,256]{1,0:T(8,128)(2,1)}, bf16[1536,256]{1,0:T(8,128)(2,1)S(1)}, u32[]{:S(2)}, u32[]{:S(2)}) collective-permute-start(bf16[1536,256]{1,0:T(8,128)(2,1)} %get-tuple-element.26), channel_id=1, source_target_pairs={{0,48},{48,0},{1,49},{49,1},{2,50},{50,2},{3,51},{51,3},{4,52},{52... | collective-permute-start | bytes 2359304 | tf_op jit(solution)/shard_map/ppermute | solution.py:299
  33.2 2.4 %collective-permute-start.1 = (bf16[256,384]{1,0:T(8,128)(2,1)}, bf16[256,384]{1,0:T(8,128)(2,1)S(1)}, u32[]{:S(2)}, u32[]{:S(2)}) collective-permute-start(bf16[256,384]{1,0:T(8,128)(2,1)} %get-tuple-element.27.ho), channel_id=1, source_target_pairs={{0,48},{48,0},{1,49},{49,1},{2,50},{50,2},{3,51},{51,3},{4,52},{52... | collective-permute-start | bytes 589832 | tf_op jit(solution)/shard_map/ppermute | solution.py:299
  35.7 1.3 collective-permute-done.1.hp
  36.9 0.7 copy-done.7
  37.6 6.4 %all-to-all-done = bf16[12,16,1024]{2,1,0:T(8,128)(2,1)S(1)} async-done(((bf16[12,16,1024]{2,1,0:T(8,128)(2,1)}), bf16[12,16,1024]{2,1,0:T(8,128)(2,1)S(1)}, u32[]{:S(2)}, u32[]{:S(2)}) %all-to-all-start) | async-done | bytes 393248 | tf_op jit(solution)/shard_map/all_to_all | solution.py:267
  44.0 2.7 %collective-permute-start.2 = (bf16[192,1024]{1,0:T(8,128)(2,1)S(1)}, bf16[192,1024]{1,0:T(8,128)(2,1)S(1)}, u32[]{:S(2)}, u32[]{:S(2)}) collective-permute-start(bf16[192,1024]{1,0:T(8,128)(2,1)S(1)} %bitcast.8), channel_id=1, source_target_pairs={{0,3},{1,0},{2,1},{3,2},{4,7},{5,4},{6,5},{7,6},{8,11},{9,8},{10,9... | collective-permute-start | bytes 1179656 | tf_op jit(solution)/shard_map/ppermute | solution.py:302
  46.7 3.0 %collective-permute-start.3 = (bf16[192,1024]{1,0:T(8,128)(2,1)S(1)}, bf16[192,1024]{1,0:T(8,128)(2,1)S(1)}, u32[]{:S(2)}, u32[]{:S(2)}) collective-permute-start(bf16[192,1024]{1,0:T(8,128)(2,1)S(1)} %bitcast.9), channel_id=1, source_target_pairs={{0,2},{1,3},{2,0},{3,1},{4,6},{5,7},{6,4},{7,5},{8,10},{9,11},{10,... | collective-permute-start | bytes 1179656 | tf_op jit(solution)/shard_map/ppermute | solution.py:302
  49.7 4.0 %collective-permute-start.4 = (bf16[192,1024]{1,0:T(8,128)(2,1)S(1)}, bf16[192,1024]{1,0:T(8,128)(2,1)S(1)}, u32[]{:S(2)}, u32[]{:S(2)}) collective-permute-start(bf16[192,1024]{1,0:T(8,128)(2,1)S(1)} %bitcast.10), channel_id=1, source_target_pairs={{0,1},{1,2},{2,3},{3,0},{4,5},{5,6},{6,7},{7,4},{8,9},{9,10},{10,1... | collective-permute-start | bytes 1179656 | tf_op jit(solution)/shard_map/ppermute | solution.py:302
  53.7 11.2 %collective-permute-done.2.refs_1_ = bf16[192,1024]{1,0:T(8,128)(2,1)S(1)} collective-permute-done((bf16[192,1024]{1,0:T(8,128)(2,1)S(1)}, bf16[192,1024]{1,0:T(8,128)(2,1)S(1)}, u32[]{:S(2)}, u32[]{:S(2)}) %collective-permute-start.2) | collective-permute-done | bytes 393248 | tf_op jit(solution)/shard_map/ppermute | solution.py:302
  65.0 1.0 copy-done.4
  66.0 1.0 copy-done.5
  67.0 0.4 shard_map.88
  67.4 0.1 collective-permute-done.4.refs_3_
  67.5 2.9 %shard_map.89 = (bf16[2304,256]{1,0:T(8,128)(2,1)S(1)}, bf16[1536,256]{1,0:T(8,128)(2,1)S(1)}) custom-call(s32[2]{0:T(128)S(1)} %copy-done.10, bf16[192,1024]{1,0:T(8,128)(2,1)S(1)} %bitcast.11, bf16[192,1024]{1,0:T(8,128)(2,1)S(1)} %collective-permute-done.2.refs_1_, bf16[192,1024]{1,0:T(8,128)(2,1)S(1)} %collective-permute-done.3.refs_2_, ...), custom_call_target="tpu_custom_call" | custom-call | flops 1006632960 | bytes 6488064 | tf_op jit(solution)/shard_map/pallas_call | solution.py:321
  70.5 2.1 %collective-permute-start.5 = (bf16[2304,256]{1,0:T(8,128)(2,1)S(1)}, bf16[2304,256]{1,0:T(8,128)(2,1)S(1)}, u32[]{:S(2)}, u32[]{:S(2)}) collective-permute-start(bf16[2304,256]{1,0:T(8,128)(2,1)S(1)} %get-tuple-element.36.ship_ref.ship), channel_id=1, source_target_pairs={{0,48},{48,0},{1,49},{49,1},{2,50},{50,2},{3,51},{51,3},{4,52},{52... | collective-permute-start | bytes 3538952 | tf_op jit(solution)/shard_map/ppermute | solution.py:299
  72.6 1.8 %shard_map.90 = (bf16[64,3072]{1,0:T(8,128)(2,1)S(1)}, bf16[64,3072]{1,0:T(8,128)(2,1)S(1)}, bf16[64,3072]{1,0:T(8,128)(2,1)S(1)}, bf16[64,3072]{1,0:T(8,128)(2,1)S(1)}) custom-call(bf16[2304,256]{1,0:T(8,128)(2,1)S(1)} %get-tuple-element.36.ship_ref.ship, bf16[384,3072]{1,0:T(8,128)(2,1)S(1)} %copy-done.1, bf16[384,3072]{1,0:T(8,128)(2,1)S(1)} %copy-done.2), custom_call_target="tpu_custom_call" | custom-call | flops 1207959552 | bytes 6291456 | tf_op jit(solution)/shard_map/pallas_call | solution.py:331
  74.4 1.0 collective-permute-done.5.got
  75.4 3.2 %shard_map.93 = bf16[8,3,192,384]{3,2,1,0:T(8,128)(2,1)} custom-call(bf16[1536,256]{1,0:T(8,128)(2,1)S(1)} %copy-done.3, bf16[1536,256]{1,0:T(8,128)(2,1)S(1)} %collective-permute-done.xp, bf16[1536,256]{1,0:T(8,128)(2,1)S(1)} %get-tuple-element.47.yo, bf16[2304,256]{1,0:T(8,128)(2,1)S(1)} %get-tuple-element.36.ship_ref.ship, ...), custom_call_target="tpu_custom_call" | custom-call | flops 1811939328 | bytes 6684672 | tf_op jit(solution)/shard_map/pallas_call | solution.py:341
  78.6 0.0 reduce-scatter.2.cloned.1.call-update
  78.6 4.5 %collective-permute-start.6 = (bf16[64,3072]{1,0:T(8,128)(2,1)S(1)}, bf16[64,3072]{1,0:T(8,128)(2,1)S(1)}, u32[]{:S(2)}, u32[]{:S(2)}) collective-permute-start(bf16[64,3072]{1,0:T(8,128)(2,1)S(1)} %get-tuple-element.42), channel_id=1, source_target_pairs={{0,1},{1,2},{2,3},{3,0},{4,5},{5,6},{6,7},{7,4},{8,9},{9,10},{10,1... | collective-permute-start | bytes 1179656 | tf_op jit(solution)/shard_map/ppermute | solution.py:302
  83.1 1.9 %collective-permute-start.7 = (bf16[64,3072]{1,0:T(8,128)(2,1)S(1)}, bf16[64,3072]{1,0:T(8,128)(2,1)S(1)}, u32[]{:S(2)}, u32[]{:S(2)}) collective-permute-start(bf16[64,3072]{1,0:T(8,128)(2,1)S(1)} %get-tuple-element.43), channel_id=1, source_target_pairs={{0,3},{1,0},{2,1},{3,2},{4,7},{5,4},{6,5},{7,6},{8,11},{9,8},{10,9... | collective-permute-start | bytes 1179656 | tf_op jit(solution)/shard_map/ppermute | solution.py:302
  85.1 3.4 %collective-permute-start.8 = (bf16[64,3072]{1,0:T(8,128)(2,1)S(1)}, bf16[64,3072]{1,0:T(8,128)(2,1)S(1)}, u32[]{:S(2)}, u32[]{:S(2)}) collective-permute-start(bf16[64,3072]{1,0:T(8,128)(2,1)S(1)} %get-tuple-element.44), channel_id=1, source_target_pairs={{0,2},{1,3},{2,0},{3,1},{4,6},{5,7},{6,4},{7,5},{8,10},{9,11},{10,... | collective-permute-start | bytes 1179656 | tf_op jit(solution)/shard_map/ppermute | solution.py:302
  88.4 11.8 %collective-permute-done.6.refs_1_ = bf16[64,3072]{1,0:T(8,128)(2,1)S(1)} collective-permute-done((bf16[64,3072]{1,0:T(8,128)(2,1)S(1)}, bf16[64,3072]{1,0:T(8,128)(2,1)S(1)}, u32[]{:S(2)}, u32[]{:S(2)}) %collective-permute-start.6) | collective-permute-done | bytes 393248 | tf_op jit(solution)/shard_map/ppermute | solution.py:302
  100.2 5.3 %collective-permute-done.7.refs_2_ = bf16[64,3072]{1,0:T(8,128)(2,1)S(1)} collective-permute-done((bf16[64,3072]{1,0:T(8,128)(2,1)S(1)}, bf16[64,3072]{1,0:T(8,128)(2,1)S(1)}, u32[]{:S(2)}, u32[]{:S(2)}) %collective-permute-start.7) | collective-permute-done | bytes 393248 | tf_op jit(solution)/shard_map/ppermute | solution.py:302
  105.5 0.5 shard_map.91
  106.1 24.1 %all_to_all.10.back_ref = bf16[12,16,1024]{2,1,0:T(8,128)(2,1)S(1)} all-to-all(bf16[12,16,1024]{2,1,0:T(8,128)(2,1)S(1)} %shard_map.91), channel_id=1, replica_groups=mesh['y'=8,'c'=2,'z'=12,'x'=4] {'z'}, dimensions={0} | all-to-all | bytes 786432 | tf_op jit(solution)/shard_map/all_to_all | solution.py:365
  130.2 1.4 shard_map.92
  (23 shorter events, 0.0 us)
Async XLA Ops:
  9.0 34.9 %all-to-all-start = ((bf16[12,16,1024]{2,1,0:T(8,128)(2,1)}), bf16[12,16,1024]{2,1,0:T(8,128)(2,1)S(1)}, u32[]{:S(2)}, u32[]{:S(2)}) async-start(bf16[12,16,1024]{2,1,0:T(8,128)(2,1)} %shard_map.86), calls=%async_computation | async-start | bytes 786432 | tf_op jit(solution)/shard_map/all_to_all | solution.py:267
  24.2 107.3 %reduce-scatter.2.cloned.1.call-start = ((), (), s32[]{:S(2)}) async-start(), calls=%async_computation.3 | async-start | bytes 3981312 | tf_op jit(solution)/shard_map/reduce_scatter | solution.py:351
  24.8 42.7 %copy-start = (bf16[384,3072]{1,0:T(8,128)(2,1)S(1)}, bf16[384,3072]{1,0:T(8,128)(2,1)}, u32[]{:S(2)}) copy-start(bf16[384,3072]{1,0:T(8,128)(2,1)} %refs_4_.1) | copy-start | bytes 7077892
  24.8 42.7 %copy-start.10 = (s32[2]{0:T(128)S(1)}, s32[2]{0:T(128)}, u32[]{:S(2)}) copy-start(s32[2]{0:T(128)} %pad_add_fusion.where_ref) | copy-start | bytes 28
  31.3 6.3 %collective-permute-start = (bf16[1536,256]{1,0:T(8,128)(2,1)}, bf16[1536,256]{1,0:T(8,128)(2,1)S(1)}, u32[]{:S(2)}, u32[]{:S(2)}) collective-permute-start(bf16[1536,256]{1,0:T(8,128)(2,1)} %get-tuple-element.26), channel_id=1, source_target_pairs={{0,48},{48,0},{1,49},{49,1},{2,50},{50,2},{3,51},{51,3},{4,52},{52... | collective-permute-start | bytes 2359304 | tf_op jit(solution)/shard_map/ppermute | solution.py:299
  33.2 3.7 %collective-permute-start.1 = (bf16[256,384]{1,0:T(8,128)(2,1)}, bf16[256,384]{1,0:T(8,128)(2,1)S(1)}, u32[]{:S(2)}, u32[]{:S(2)}) collective-permute-start(bf16[256,384]{1,0:T(8,128)(2,1)} %get-tuple-element.27.ho), channel_id=1, source_target_pairs={{0,48},{48,0},{1,49},{49,1},{2,50},{50,2},{3,51},{51,3},{4,52},{52... | collective-permute-start | bytes 589832 | tf_op jit(solution)/shard_map/ppermute | solution.py:299
  36.9 0.7 copy-start.7
  44.0 21.0 %collective-permute-start.2 = (bf16[192,1024]{1,0:T(8,128)(2,1)S(1)}, bf16[192,1024]{1,0:T(8,128)(2,1)S(1)}, u32[]{:S(2)}, u32[]{:S(2)}) collective-permute-start(bf16[192,1024]{1,0:T(8,128)(2,1)S(1)} %bitcast.8), channel_id=1, source_target_pairs={{0,3},{1,0},{2,1},{3,2},{4,7},{5,4},{6,5},{7,6},{8,11},{9,8},{10,9... | collective-permute-start | bytes 1179656 | tf_op jit(solution)/shard_map/ppermute | solution.py:302
  46.7 20.7 %collective-permute-start.3 = (bf16[192,1024]{1,0:T(8,128)(2,1)S(1)}, bf16[192,1024]{1,0:T(8,128)(2,1)S(1)}, u32[]{:S(2)}, u32[]{:S(2)}) collective-permute-start(bf16[192,1024]{1,0:T(8,128)(2,1)S(1)} %bitcast.9), channel_id=1, source_target_pairs={{0,2},{1,3},{2,0},{3,1},{4,6},{5,7},{6,4},{7,5},{8,10},{9,11},{10,... | collective-permute-start | bytes 1179656 | tf_op jit(solution)/shard_map/ppermute | solution.py:302
  49.7 17.8 %collective-permute-start.4 = (bf16[192,1024]{1,0:T(8,128)(2,1)S(1)}, bf16[192,1024]{1,0:T(8,128)(2,1)S(1)}, u32[]{:S(2)}, u32[]{:S(2)}) collective-permute-start(bf16[192,1024]{1,0:T(8,128)(2,1)S(1)} %bitcast.10), channel_id=1, source_target_pairs={{0,1},{1,2},{2,3},{3,0},{4,5},{5,6},{6,7},{7,4},{8,9},{9,10},{10,1... | collective-permute-start | bytes 1179656 | tf_op jit(solution)/shard_map/ppermute | solution.py:302
  65.0 1.0 copy-start.4
  66.0 1.0 copy-start.5
  67.5 5.0 %copy-start.1 = (bf16[384,3072]{1,0:T(8,128)(2,1)S(1)}, bf16[384,3072]{1,0:T(8,128)(2,1)}, u32[]{:S(2)}) copy-start(bf16[384,3072]{1,0:T(8,128)(2,1)} %wg_ref.1) | copy-start | bytes 7077892
  67.5 5.0 %copy-start.2 = (bf16[384,3072]{1,0:T(8,128)(2,1)S(1)}, bf16[384,3072]{1,0:T(8,128)(2,1)}, u32[]{:S(2)}) copy-start(bf16[384,3072]{1,0:T(8,128)(2,1)} %wu_ref.1) | copy-start | bytes 7077892
  70.5 4.9 %copy-start.3 = (bf16[1536,256]{1,0:T(8,128)(2,1)S(1)}, bf16[1536,256]{1,0:T(8,128)(2,1)}, u32[]{:S(2)}) copy-start(bf16[1536,256]{1,0:T(8,128)(2,1)} %get-tuple-element.45.xo) | copy-start | bytes 2359300
  70.5 4.9 %copy-start.6 = (bf16[256,384]{1,0:T(8,128)(2,1)S(1)}, bf16[256,384]{1,0:T(8,128)(2,1)}, u32[]{:S(2)}) copy-start(bf16[256,384]{1,0:T(8,128)(2,1)} %get-tuple-element.27.ho) | copy-start | bytes 589828
  70.5 4.9 %copy-start.8 = (bf16[256,384]{1,0:T(8,128)(2,1)S(1)}, bf16[256,384]{1,0:T(8,128)(2,1)}, u32[]{:S(2)}) copy-start(bf16[256,384]{1,0:T(8,128)(2,1)} %copy-done.7) | copy-start | bytes 589828
  70.5 4.9 %collective-permute-start.5 = (bf16[2304,256]{1,0:T(8,128)(2,1)S(1)}, bf16[2304,256]{1,0:T(8,128)(2,1)S(1)}, u32[]{:S(2)}, u32[]{:S(2)}) collective-permute-start(bf16[2304,256]{1,0:T(8,128)(2,1)S(1)} %get-tuple-element.36.ship_ref.ship), channel_id=1, source_target_pairs={{0,48},{48,0},{1,49},{49,1},{2,50},{50,2},{3,51},{51,3},{4,52},{52... | collective-permute-start | bytes 3538952 | tf_op jit(solution)/shard_map/ppermute | solution.py:299
  78.6 51.6 %copy-start.9 = (s32[10,2]{0,1:T(2,128)S(1)}, s32[10,2]{0,1:T(2,128)}, u32[]{:S(2)}) copy-start(s32[10,2]{0,1:T(2,128)} %param.8) | copy-start | bytes 244
  78.6 21.7 %collective-permute-start.6 = (bf16[64,3072]{1,0:T(8,128)(2,1)S(1)}, bf16[64,3072]{1,0:T(8,128)(2,1)S(1)}, u32[]{:S(2)}, u32[]{:S(2)}) collective-permute-start(bf16[64,3072]{1,0:T(8,128)(2,1)S(1)} %get-tuple-element.42), channel_id=1, source_target_pairs={{0,1},{1,2},{2,3},{3,0},{4,5},{5,6},{6,7},{7,4},{8,9},{9,10},{10,1... | collective-permute-start | bytes 1179656 | tf_op jit(solution)/shard_map/ppermute | solution.py:302
  83.1 22.4 %collective-permute-start.7 = (bf16[64,3072]{1,0:T(8,128)(2,1)S(1)}, bf16[64,3072]{1,0:T(8,128)(2,1)S(1)}, u32[]{:S(2)}, u32[]{:S(2)}) collective-permute-start(bf16[64,3072]{1,0:T(8,128)(2,1)S(1)} %get-tuple-element.43), channel_id=1, source_target_pairs={{0,3},{1,0},{2,1},{3,2},{4,7},{5,4},{6,5},{7,6},{8,11},{9,8},{10,9... | collective-permute-start | bytes 1179656 | tf_op jit(solution)/shard_map/ppermute | solution.py:302
  85.1 20.5 %collective-permute-start.8 = (bf16[64,3072]{1,0:T(8,128)(2,1)S(1)}, bf16[64,3072]{1,0:T(8,128)(2,1)S(1)}, u32[]{:S(2)}, u32[]{:S(2)}) collective-permute-start(bf16[64,3072]{1,0:T(8,128)(2,1)S(1)} %get-tuple-element.44), channel_id=1, source_target_pairs={{0,2},{1,3},{2,0},{3,1},{4,6},{5,7},{6,4},{7,5},{8,10},{9,11},{10,... | collective-permute-start | bytes 1179656 | tf_op jit(solution)/shard_map/ppermute | solution.py:302
Sparse Core Ops, SparseCore 0:
  78.7 50.6 reduce-scatter.1
